TPU v7x, 128 devices: a whole 4x4x4 slice. The times are simulated.
128 devices in a mesh: dp: 4 (over x), block: 32 (over z, y, core).
Axes of the slice: x: 4, y: 4, z: 4, core: 2. Of those that a mesh axis runs over, the one named last changes fastest.
Arguments:
- tokens: bfloat16 [16384, 8192], P('dp', 'block'), may hold values from -6 to 6
- cotangent: bfloat16 [16384, 8192], P('dp', 'block'), may hold values from -0.09375 to 0.09375
- first_mean: float32 [64, 128, 128], P('block', 'dp'), may hold values from -0.5 to 0.5
- first_rho: float32 [64, 128, 128], P('block', 'dp'), may hold values from -4 to -2
- first_noise: float32 [64, 128, 128], P('block', 'dp'), may hold values from -6 to 6
- second_mean: float32 [128, 64, 512], P('block', 'dp'), may hold values from -0.75 to 0.75
- second_rho: float32 [128, 64, 512], P('block', 'dp'), may hold values from -4 to -2
- second_noise: float32 [128, 64, 512], P('block', 'dp'), may hold values from -6 to 6
- third_mean: float32 [128, 256, 64], P('block', 'dp'), may hold values from -0.375 to 0.375
- third_rho: float32 [128, 256, 64], P('block', 'dp'), may hold values from -4 to -2
- third_noise: float32 [128, 256, 64], P('block', 'dp'), may hold values from -6 to 6
- fourth_mean: float32 [64, 128, 128], P('block', 'dp'), may hold values from -0.5 to 0.5
- fourth_rho: float32 [64, 128, 128], P('block', 'dp'), may hold values from -4 to -2
- fourth_noise: float32 [64, 128, 128], P('block', 'dp'), may hold values from -6 to 6
Outputs:
- layer_out: bfloat16 [16384, 8192], P('dp', 'block')
- first_mean_grad: float32 [64, 128, 128], P('block', 'dp')
- first_rho_grad: float32 [64, 128, 128], P('block', 'dp')
- second_mean_grad: float32 [128, 64, 512], P('block', 'dp')
- second_rho_grad: float32 [128, 64, 512], P('block', 'dp')
- third_mean_grad: float32 [128, 256, 64], P('block', 'dp')
- third_rho_grad: float32 [128, 256, 64], P('block', 'dp')
- fourth_mean_grad: float32 [64, 128, 128], P('block', 'dp')
- fourth_rho_grad: float32 [64, 128, 128], P('block', 'dp')
All inputs are finite; a program needn't handle non-finite values.
Results may differ from a plain program's by a relative error of at most 0.01.
Values may be sent and summed in bfloat16 or wider, within the bound.
No kernel may reach another device: no remote copies, remote signals or barrier semaphores. Data moves between devices by JAX's collectives and lax.ppermute only.
A program may use at most 192 MiB of HBM per device.

v0:
```python
import jax
import jax.numpy as jnp
from jax import lax
from jax.sharding import PartitionSpec as P


def sampled(mean, rho, noise):
    return (mean + jax.nn.softplus(rho) * noise).astype(jnp.bfloat16)


def permute(blocks):
    return lax.all_to_all(blocks, "block", split_axis=0, concat_axis=1, tiled=True)


def reduce_share(term):
    return lax.psum_scatter(term, "dp", scatter_dimension=1, tiled=True)


def shards(
    tokens,
    cotangent,
    first_mean,
    first_rho,
    first_noise,
    second_mean,
    second_rho,
    second_noise,
    third_mean,
    third_rho,
    third_noise,
    fourth_mean,
    fourth_rho,
    fourth_noise,
):
    local_one = sampled(first_mean, first_rho, first_noise)
    local_two = sampled(second_mean, second_rho, second_noise)
    local_three = sampled(third_mean, third_rho, third_noise)
    local_four = sampled(fourth_mean, fourth_rho, fourth_noise)
    weight_one, weight_two, weight_three, weight_four = (
        lax.all_gather(local_one, "dp", axis=1, tiled=True),
        lax.all_gather(local_two, "dp", axis=1, tiled=True),
        lax.all_gather(local_three, "dp", axis=1, tiled=True),
        lax.all_gather(local_four, "dp", axis=1, tiled=True),
    )
    count = tokens.shape[0]
    owned = weight_one.shape[0]
    width = weight_one.shape[1]
    hidden_half = weight_three.shape[1]
    inputs = tokens.reshape(count, owned, width)
    first_out = jnp.einsum(
        "tma,mac->cmt", inputs, weight_one, preferred_element_type=jnp.float32
    ).astype(jnp.bfloat16)
    permuted = permute(first_out)
    gate_up = jnp.einsum("cmt,cme->cte", permuted, weight_two, preferred_element_type=jnp.float32)
    gate = gate_up[..., :hidden_half]
    upward = gate_up[..., hidden_half:]
    hidden = (jax.nn.silu(gate) * upward).astype(jnp.bfloat16)
    third_out = jnp.einsum(
        "ctk,ckm->mct", hidden, weight_three, preferred_element_type=jnp.float32
    ).astype(jnp.bfloat16)
    returned = permute(third_out)
    layer_out = (
        jnp.einsum("mct,mcd->tmd", returned, weight_four, preferred_element_type=jnp.float32)
        .astype(jnp.bfloat16)
        .reshape(count, owned * width)
    )
    upstream = cotangent.reshape(count, owned, width)
    back_four = jnp.einsum(
        "tmd,mcd->cmt", upstream, weight_four, preferred_element_type=jnp.float32
    ).astype(jnp.bfloat16)
    term_four = jnp.einsum("mct,tmd->mcd", returned, upstream, preferred_element_type=jnp.float32)
    share_four = reduce_share(term_four)
    back_three = permute(back_four)
    hidden_grad = jnp.einsum(
        "cmt,ckm->ctk", back_three, weight_three, preferred_element_type=jnp.float32
    )
    term_three = jnp.einsum("ctk,cmt->ckm", hidden, back_three, preferred_element_type=jnp.float32)
    share_three = reduce_share(term_three)
    sigma_gate = jax.nn.sigmoid(gate)
    gate_grad = hidden_grad * upward * sigma_gate * (1.0 + gate * (1.0 - sigma_gate))
    up_grad = hidden_grad * jax.nn.silu(gate)
    pair_grad = jnp.concatenate([gate_grad, up_grad], axis=-1).astype(jnp.bfloat16)
    back_two = jnp.einsum(
        "cte,cme->mct", pair_grad, weight_two, preferred_element_type=jnp.float32
    ).astype(jnp.bfloat16)
    term_two = jnp.einsum("cmt,cte->cme", permuted, pair_grad, preferred_element_type=jnp.float32)
    share_two = reduce_share(term_two)
    back_one = permute(back_two)
    term_one = jnp.einsum("tma,mct->mac", inputs, back_one, preferred_element_type=jnp.float32)
    share_one = reduce_share(term_one)
    return (
        layer_out,
        share_one,
        share_one * first_noise * jax.nn.sigmoid(first_rho),
        share_two,
        share_two * second_noise * jax.nn.sigmoid(second_rho),
        share_three,
        share_three * third_noise * jax.nn.sigmoid(third_rho),
        share_four,
        share_four * fourth_noise * jax.nn.sigmoid(fourth_rho),
    )


def solution(mesh):
    in_specs = (
        P("dp", "block"),
        P("dp", "block"),
        P("block", "dp", None),
        P("block", "dp", None),
        P("block", "dp", None),
        P("block", "dp", None),
        P("block", "dp", None),
        P("block", "dp", None),
        P("block", "dp", None),
        P("block", "dp", None),
        P("block", "dp", None),
        P("block", "dp", None),
        P("block", "dp", None),
        P("block", "dp", None),
    )
    out_specs = (
        P("dp", "block"),
        P("block", "dp", None),
        P("block", "dp", None),
        P("block", "dp", None),
        P("block", "dp", None),
        P("block", "dp", None),
        P("block", "dp", None),
        P("block", "dp", None),
        P("block", "dp", None),
    )
    return jax.shard_map(shards, mesh=mesh, in_specs=in_specs, out_specs=out_specs, check_vma=False)
```

profile of v0, /device:TPU:0, one launch (start us, length us, event | category | flops | bytes accessed | tf_op | source)
XLA Modules:
  0.0 309.9 jit_solution(7051821593120460489)
XLA Ops:
  8.2 12.3 %all_gather.14 = bf16[2,128,128]{2,1,0:T(8,128)(2,1)S(1)} all-gather(bf16[2,32,128]{2,1,0:T(8,128)(2,1)S(1)} %fusion.35), channel_id=1, replica_groups=mesh['dp'=4,'block'=32] {'dp'}, dimensions={1}, use_global_device_ids=true | all-gather | bytes 81920 | tf_op jit(solution)/shard_map/all_gather | solution.py:40
  24.7 8.6 %all-to-all-start = ((bf16[128,2,4096]{2,1,0:T(2,128)(2,1)}), bf16[128,2,4096]{2,1,0:T(2,128)(2,1)}, u32[]{:S(2)}, u32[]{:S(2)}) async-start(bf16[128,2,4096]{2,1,0:T(2,128)(2,1)} %copy.89), calls=%async_computation | async-start | bytes 4194304 | tf_op jit(solution)/shard_map/all_to_all | solution.py:12
  33.4 11.9 %all_gather.12 = bf16[2,128,128]{2,1,0:T(8,128)(2,1)S(1)} all-gather(bf16[2,32,128]{2,1,0:T(8,128)(2,1)S(1)} %fusion.32), channel_id=1, replica_groups=mesh['dp'=4,'block'=32] {'dp'}, dimensions={1}, use_global_device_ids=true | all-gather | bytes 81920 | tf_op jit(solution)/shard_map/all_gather | solution.py:43
  51.1 12.2 %all-to-all-done = bf16[128,2,4096]{2,1,0:T(2,128)(2,1)} async-done(((bf16[128,2,4096]{2,1,0:T(2,128)(2,1)}), bf16[128,2,4096]{2,1,0:T(2,128)(2,1)}, u32[]{:S(2)}, u32[]{:S(2)}) %all-to-all-start) | async-done | bytes 2097184 | tf_op jit(solution)/shard_map/all_to_all | solution.py:12
  63.3 4.8 %all-to-all-start.2 = ((bf16[128,2,4096]{2,1,0:T(2,128)(2,1)}), bf16[128,2,4096]{2,1,0:T(2,128)(2,1)}, u32[]{:S(2)}, u32[]{:S(2)}) async-start(bf16[128,2,4096]{2,1,0:T(2,128)(2,1)} %copy.96), calls=%async_computation.2 | async-start | bytes 4194304 | tf_op jit(solution)/shard_map/all_to_all | solution.py:12
  68.3 12.3 %all_gather.13 = bf16[4,256,64]{2,0,1:T(4,128)(2,1)S(1)} all-gather(bf16[4,64,64]{2,0,1:T(4,128)(2,1)S(1)} %copy.87), channel_id=1, replica_groups=mesh['dp'=4,'block'=32] {'dp'}, dimensions={1}, use_global_device_ids=true | all-gather | bytes 163840 | tf_op jit(solution)/shard_map/all_gather | solution.py:42
  80.6 12.4 %all_gather.15 = bf16[4,64,512]{2,1,0:T(8,128)(2,1)S(1)} all-gather(bf16[4,16,512]{2,1,0:T(8,128)(2,1)S(1)} %fusion.29), channel_id=1, replica_groups=mesh['dp'=4,'block'=32] {'dp'}, dimensions={1}, use_global_device_ids=true | all-gather | bytes 327680 | tf_op jit(solution)/shard_map/all_gather | solution.py:41
  93.1 5.5 %copy.172 = bf16[32,4,2,4096]{3,2,0,1:T(2,128)(2,1)} copy(bf16[32,4,2,4096]{3,2,1,0:T(2,128)(2,1)} %bitcast.1) | data formatting | bytes 4194304 | tf_op jit(solution)/shard_map/all_to_all | solution.py:12
  98.6 4.1 %all_to_all.55 = bf16[4,64,4096]{2,1,0:T(8,128)(2,1)} reshape(bf16[4,32,2,4096]{3,2,1,0:T(2,128)(2,1)} %bitcast.71) | data formatting | bytes 4194304 | tf_op jit(solution)/shard_map/all_to_all | solution.py:12
  102.7 5.5 %copy.170 = bf16[32,4,2,4096]{3,2,0,1:T(2,128)(2,1)} copy(bf16[32,4,2,4096]{3,2,1,0:T(2,128)(2,1)} %bitcast.9) | data formatting | bytes 4194304 | tf_op jit(solution)/shard_map/all_to_all | solution.py:12
  108.2 4.1 %all_to_all.63 = bf16[4,64,4096]{2,1,0:T(8,128)(2,1)} reshape(bf16[4,32,2,4096]{3,2,1,0:T(2,128)(2,1)} %bitcast.72) | data formatting | bytes 4194304 | tf_op jit(solution)/shard_map/all_to_all | solution.py:12
  112.3 14.8 %fusion.42 = f32[4,4096,512]{1,2,0:T(8,128)} fusion(bf16[4,64,4096]{2,1,0:T(8,128)(2,1)} %all_to_all.55, bf16[4,64,512]{2,1,0:T(8,128)(2,1)S(1)} %all_gather.15), kind=kOutput, calls=%fused_computation.67 | convolution fusion | flops 1073741824 | bytes 35913728 | tf_op jit(solution)/shard_map/cmt,cme->cte/dot_general | solution.py:54
  127.2 21.0 %multiply_convert_fusion.1 = (bf16[4,4096,256]{1,2,0:T(8,128)(2,1)}, bf16[4,4096,256]{1,2,0:T(8,128)(2,1)}, bf16[4,4096,256]{1,2,0:T(8,128)(2,1)}) fusion(f32[4,4096,512]{1,2,0:T(8,128)} %fusion.42, bf16[4,64,4096]{2,1,0:T(8,128)(2,1)S(1)} %copy-done.1, bf16[4,256,64]{2,0,1:T(4,128)(2,1)S(1)} %all_gather.13), kind=kOutput, calls=%fused_computation.2 | convolution fusion | flops 599785472 | bytes 60948480 | tf_op jit(solution)/shard_map/cmt,ckm->ctk/dot_general | solution.py:74
  148.2 7.5 %fusion.4 = bf16[64,4,4096]{2,0,1:T(8,128)(2,1)S(1)} fusion(bf16[4,64,512]{2,1,0:T(8,128)(2,1)S(1)} %all_gather.15, bf16[4,4096,256]{1,2,0:T(8,128)(2,1)} %get-tuple-element.43, bf16[4,4096,256]{1,2,0:T(8,128)(2,1)} %get-tuple-element.42), kind=kOutput, calls=%fused_computation.13 | convolution fusion | flops 1108344832 | bytes 19136512 | tf_op jit(solution)/shard_map/cte,cme->mct/dot_general | solution.py:83
  158.6 7.5 %all-to-all-start.3 = ((bf16[64,4,4096]{2,1,0:T(4,128)(2,1)}), bf16[64,4,4096]{2,1,0:T(4,128)(2,1)}, u32[]{:S(2)}, u32[]{:S(2)}) async-start(bf16[64,4,4096]{2,1,0:T(4,128)(2,1)} %copy.100), calls=%async_computation.3 | async-start | bytes 4194304 | tf_op jit(solution)/shard_map/all_to_all | solution.py:12
  166.2 5.0 %fusion.7 = bf16[64,4,4096]{2,0,1:T(8,128)(2,1)S(1)} fusion(bf16[4,4096,256]{1,2,0:T(8,128)(2,1)} %get-tuple-element.44, bf16[4,256,64]{2,0,1:T(4,128)(2,1)S(1)} %all_gather.13), kind=kOutput, calls=%fused_computation.16 | convolution fusion | flops 537919488 | bytes 10616832 | tf_op jit(solution)/shard_map/ctk,ckm->mct/dot_general | solution.py:58
  174.1 6.5 %fusion.43 = f32[4,256,64]{2,1,0:T(8,128)} fusion(bf16[4,4096,256]{1,2,0:T(8,128)(2,1)} %get-tuple-element.44, bf16[4,64,4096]{2,1,0:T(8,128)(2,1)S(1)} %copy-done.2), kind=kOutput, calls=%fused_computation.68 | convolution fusion | flops 536870912 | bytes 10747904 | tf_op jit(solution)/shard_map/ctk,cmt->ckm/dot_general | solution.py:77
  180.6 15.4 %all-to-all-done.3 = bf16[64,4,4096]{2,1,0:T(4,128)(2,1)} async-done(((bf16[64,4,4096]{2,1,0:T(4,128)(2,1)}), bf16[64,4,4096]{2,1,0:T(4,128)(2,1)}, u32[]{:S(2)}, u32[]{:S(2)}) %all-to-all-start.3) | async-done | bytes 2097184 | tf_op jit(solution)/shard_map/all_to_all | solution.py:12
  196.1 4.8 %all-to-all-start.1 = ((bf16[64,4,4096]{2,1,0:T(4,128)(2,1)}), bf16[64,4,4096]{2,1,0:T(4,128)(2,1)}, u32[]{:S(2)}, u32[]{:S(2)}) async-start(bf16[64,4,4096]{2,1,0:T(4,128)(2,1)} %copy.93), calls=%async_computation.1 | async-start | bytes 4194304 | tf_op jit(solution)/shard_map/all_to_all | solution.py:12
  200.9 10.0 %fusion.1 = f32[4,64,512]{2,1,0:T(8,128)} fusion(bf16[4,64,4096]{2,1,0:T(8,128)(2,1)} %all_to_all.55, bf16[4,4096,256]{1,2,0:T(8,128)(2,1)} %get-tuple-element.43, bf16[4,4096,256]{1,2,0:T(8,128)(2,1)} %get-tuple-element.42), kind=kOutput, calls=%fused_computation.6 | convolution fusion | flops 1107296256 | bytes 19398656 | tf_op jit(solution)/shard_map/cmt,cte->cme/dot_general | solution.py:86
  214.2 18.9 %reduce-scatter.3.cloned.1.call-done = f32[4,16,512]{2,1,0:T(8,128)} async-done(((f32[4,64,512]{2,1,0:T(8,128)}), f32[4,16,512]{2,1,0:T(8,128)}) %reduce-scatter.3.cloned.1.call-update) | async-done | bytes 131088 | tf_op jit(solution)/shard_map/reduce_scatter | solution.py:16
  234.7 4.4 %copy.169 = bf16[32,2,4,4096]{3,2,0,1:T(4,128)(2,1)} copy(bf16[32,2,4,4096]{3,2,1,0:T(4,128)(2,1)} %bitcast.12) | data formatting | bytes 4194304 | tf_op jit(solution)/shard_map/all_to_all | solution.py:12
  246.1 4.5 %copy.171 = bf16[32,2,4,4096]{3,2,0,1:T(4,128)(2,1)} copy(bf16[32,2,4,4096]{3,2,1,0:T(4,128)(2,1)} %bitcast.4) | data formatting | bytes 4194304 | tf_op jit(solution)/shard_map/all_to_all | solution.py:12
  266.0 34.0 %all-reduce.5.cloned.1.call-done = (f32[2,128,128]{2,0,1:T(2,128)}, f32[2,128,128]{2,0,1:T(2,128)}) async-done(((f32[2,128,128]{2,0,1:T(2,128)}, f32[2,128,128]{2,0,1:T(2,128)}), (f32[2,128,128]{2,0,1:T(2,128)}, f32[2,128,128]{2,0,1:T(2,128)})) %all-reduce.5.cloned.1.call-update) | async-done | bytes 262160
  (66 shorter events, 47.2 us)
Async XLA Ops:
  7.2 13.3 %copy-start = (bf16[4096,256]{1,0:T(8,128)(2,1)S(1)}, bf16[4096,256]{1,0:T(8,128)(2,1)}, u32[]{:S(2)}) copy-start(bf16[4096,256]{1,0:T(8,128)(2,1)} %param.14) | copy-start | bytes 6291460
  24.7 8.6 %copy-start.9 = (f32[2,32,128]{2,1,0:T(8,128)S(1)}, f32[2,32,128]{2,1,0:T(8,128)}, u32[]{:S(2)}) copy-start(f32[2,32,128]{2,1,0:T(8,128)} %param.27) | copy-start | bytes 98308
  24.7 8.6 %copy-start.10 = (f32[2,32,128]{2,1,0:T(8,128)S(1)}, f32[2,32,128]{2,1,0:T(8,128)}, u32[]{:S(2)}) copy-start(f32[2,32,128]{2,1,0:T(8,128)} %param.26) | copy-start | bytes 98308
  24.7 8.6 %copy-start.13 = (f32[2,32,128]{2,1,0:T(8,128)S(1)}, f32[2,32,128]{2,1,0:T(8,128)}, u32[]{:S(2)}) copy-start(f32[2,32,128]{2,1,0:T(8,128)} %param.25) | copy-start | bytes 98308
  24.7 38.6 %all-to-all-start = ((bf16[128,2,4096]{2,1,0:T(2,128)(2,1)}), bf16[128,2,4096]{2,1,0:T(2,128)(2,1)}, u32[]{:S(2)}, u32[]{:S(2)}) async-start(bf16[128,2,4096]{2,1,0:T(2,128)(2,1)} %copy.89), calls=%async_computation | async-start | bytes 4194304 | tf_op jit(solution)/shard_map/all_to_all | solution.py:12
  51.1 17.0 %copy-start.3 = (f32[4,64,64]{2,1,0:T(8,128)S(1)}, f32[4,64,64]{2,1,0:T(8,128)}, u32[]{:S(2)}) copy-start(f32[4,64,64]{2,1,0:T(8,128)} %param.24) | copy-start | bytes 196612
  51.1 17.0 %copy-start.4 = (f32[4,64,64]{2,1,0:T(8,128)S(1)}, f32[4,64,64]{2,1,0:T(8,128)}, u32[]{:S(2)}) copy-start(f32[4,64,64]{2,1,0:T(8,128)} %param.23) | copy-start | bytes 196612
  51.1 17.0 %copy-start.7 = (f32[4,64,64]{2,1,0:T(8,128)S(1)}, f32[4,64,64]{2,1,0:T(8,128)}, u32[]{:S(2)}) copy-start(f32[4,64,64]{2,1,0:T(8,128)} %param.22) | copy-start | bytes 196612
  51.1 29.5 %copy-start.5 = (f32[4,16,512]{2,1,0:T(8,128)S(1)}, f32[4,16,512]{2,1,0:T(8,128)}, u32[]{:S(2)}) copy-start(f32[4,16,512]{2,1,0:T(8,128)} %param.21) | copy-start | bytes 393220
  51.1 29.5 %copy-start.6 = (f32[4,16,512]{2,1,0:T(8,128)S(1)}, f32[4,16,512]{2,1,0:T(8,128)}, u32[]{:S(2)}) copy-start(f32[4,16,512]{2,1,0:T(8,128)} %param.20) | copy-start | bytes 393220
  51.1 29.4 %copy-start.8 = (f32[4,16,512]{2,1,0:T(8,128)S(1)}, f32[4,16,512]{2,1,0:T(8,128)}, u32[]{:S(2)}) copy-start(f32[4,16,512]{2,1,0:T(8,128)} %param.19) | copy-start | bytes 393220
  63.3 39.4 %all-to-all-start.2 = ((bf16[128,2,4096]{2,1,0:T(2,128)(2,1)}), bf16[128,2,4096]{2,1,0:T(2,128)(2,1)}, u32[]{:S(2)}, u32[]{:S(2)}) async-start(bf16[128,2,4096]{2,1,0:T(2,128)(2,1)} %copy.96), calls=%async_computation.2 | async-start | bytes 4194304 | tf_op jit(solution)/shard_map/all_to_all | solution.py:12
  112.3 14.8 %copy-start.1 = (bf16[4,64,4096]{2,1,0:T(8,128)(2,1)S(1)}, bf16[4,64,4096]{2,1,0:T(8,128)(2,1)}, u32[]{:S(2)}) copy-start(bf16[4,64,4096]{2,1,0:T(8,128)(2,1)} %all_to_all.63) | copy-start | bytes 6291460
  158.6 37.5 %all-to-all-start.3 = ((bf16[64,4,4096]{2,1,0:T(4,128)(2,1)}), bf16[64,4,4096]{2,1,0:T(4,128)(2,1)}, u32[]{:S(2)}, u32[]{:S(2)}) async-start(bf16[64,4,4096]{2,1,0:T(4,128)(2,1)} %copy.100), calls=%async_computation.3 | async-start | bytes 4194304 | tf_op jit(solution)/shard_map/all_to_all | solution.py:12
  166.1 46.4 %reduce-scatter.5.cloned.1.call-start = ((), (), s32[]{:S(2)}) async-start(), calls=%async_computation.7 | async-start | bytes 655360 | tf_op jit(solution)/shard_map/reduce_scatter | solution.py:16
  171.2 3.0 copy-start.2
  196.1 50.1 %all-to-all-start.1 = ((bf16[64,4,4096]{2,1,0:T(4,128)(2,1)}), bf16[64,4,4096]{2,1,0:T(4,128)(2,1)}, u32[]{:S(2)}, u32[]{:S(2)}) async-start(bf16[64,4,4096]{2,1,0:T(4,128)(2,1)} %copy.93), calls=%async_computation.1 | async-start | bytes 4194304 | tf_op jit(solution)/shard_map/all_to_all | solution.py:12
  200.9 10.4 %copy-start.14 = (u32[128]{0:T(128)S(1)}, u32[128]{0:T(128)}, u32[]{:S(2)}) copy-start(u32[128]{0:T(128)} %constant.30) | copy-start | bytes 1540
  200.9 32.2 %reduce-scatter.3.cloned.1.call-start = ((), (), s32[]{:S(2)}) async-start(), calls=%async_computation.6 | async-start | bytes 655360 | tf_op jit(solution)/shard_map/reduce_scatter | solution.py:16
  211.0 89.0 %all-reduce.5.cloned.1.call-start = ((), (), s32[]{:S(2)}) async-start(), calls=%async_computation.8 | async-start | bytes 524288
  261.9 38.0 %copy-start.11 = (f32[2,32,128]{2,1,0:T(8,128)S(1)}, f32[2,32,128]{2,1,0:T(8,128)}, u32[]{:S(2)}) copy-start(f32[2,32,128]{2,1,0:T(8,128)} %param.18) | copy-start | bytes 98308
  261.9 38.0 %copy-start.12 = (f32[2,32,128]{2,1,0:T(8,128)S(1)}, f32[2,32,128]{2,1,0:T(8,128)}, u32[]{:S(2)}) copy-start(f32[2,32,128]{2,1,0:T(8,128)} %param.17) | copy-start | bytes 98308
Sparse Core Ops, SparseCore 0:
  180.8 21.9 reduce-scatter.4
  211.1 21.9 reduce-scatter.2
  258.4 41.4 all-reduce.4
where the time goes:
time: 311 us; the launch traced here: 310 us
  waiting for transfers between devices  80.5 us (26%)
  matrix products  76.8 us (25%)
  local copies, waits for them, and re-layouts  57.7 us (19%)
  blocking collectives  48.9 us (16%)
  starting transfers between devices  26 us (8%)
  between operations  14.6 us (5%)
  other arithmetic  5.32 us (2%)
    all_to_all x8, local copies, waits for them, and re-layouts, permute(): lax.all_to_all(blocks, 'block', split_axis=0, concat_axis=1, tiled=True)  36.1 us
    unnamed x4, waiting for transfers between devices  34 us
    all_to_all x4, waiting for transfers between devices, permute(): lax.all_to_all(blocks, 'block', split_axis=0, concat_axis=1, tiled=True)  27.6 us
    all_to_all x4, starting transfers between devices, permute(): lax.all_to_all(blocks, 'block', split_axis=0, concat_axis=1, tiled=True)  25.6 us
    dot_general x1, matrix products, shards(): jnp.einsum('cmt,ckm->ctk', back_three, weight_three, preferred_element_ty...  21 us
    reduce_scatter x2, waiting for transfers between devices, reduce_share(): return lax.psum_scatter(term, 'dp', scatter_dimension=1, tiled=True)  18.9 us
    dot_general x1, matrix products, shards(): jnp.einsum('cmt,cme->cte', permuted, weight_two, preferred_element_type=j...  14.8 us
    all_gather x1, blocking collectives, shards(): lax.all_gather(local_two, 'dp', axis=1, tiled=True)  12.4 us
  transfers between devices with their start and end apart: 7, of which 4 were waited for; matrix products, arithmetic and copies ran while one was open for 18% of the time, Pallas kernels for 0%

commit v1 on v0

v1 whole, which is shorter than its diff:
```python
import functools

import jax
import jax.numpy as jnp
from jax import lax
from jax.experimental import pallas as pl
from jax.experimental.pallas import tpu as pltpu
from jax.sharding import PartitionSpec as P

F32, BF16 = jnp.float32, jnp.bfloat16
EXACT = lax.Precision.HIGHEST
VMEM = pl.BlockSpec(memory_space=pltpu.VMEM)


def dot(a, b, ca, cb, **kw):
    return lax.dot_general(a, b, (((ca,), (cb,)), ((), ())), preferred_element_type=F32, **kw)


def sampled(mean, rho, noise):
    return (mean + jax.nn.softplus(rho) * noise).astype(BF16)


def params():
    return pltpu.CompilerParams(vmem_limit_bytes=50 * 2**20, dimension_semantics=("arbitrary",))


def gather_parts(part, n):
    return [part] + [lax.ppermute(part, "dp", [(j, (j + k) % n) for j in range(n)]) for k in range(1, n)]


def scatter_parts(parts, n):
    return [parts[0]] + [
        lax.ppermute(parts[k], "dp", [(j, (j + k) % n) for j in range(n)]) for k in range(1, n)
    ]


def exchange(x):
    return lax.all_to_all(x, "block", split_axis=0, concat_axis=0, tiled=True)


def place_m(m, owned_m, owned_c, rows, width, dtype):
    r = lax.broadcasted_iota(jnp.int32, (rows, width), 0)
    c = lax.broadcasted_iota(jnp.int32, (rows, width), 1)
    hit = (r // owned_c % owned_m == m) & (r // (owned_m * owned_c) * owned_c + r % owned_c == c)
    return jnp.where(hit, 1.0, 0.0).astype(dtype)


def place_c(c, owned_c, rows, width, dtype):
    r = lax.broadcasted_iota(jnp.int32, (rows, width), 0)
    m = lax.broadcasted_iota(jnp.int32, (rows, width), 1)
    return jnp.where((r % owned_c == c) & (r // owned_c == m), 1.0, 0.0).astype(dtype)


def owner(k, n):
    return lax.rem(lax.axis_index("dp") + (n + k), n)


def assemble(parts, full, n, first=0):
    size = parts[0].shape[1]
    for k in range(n):
        at = pl.multiple_of(owner(-k, n) * size, size)
        for i in range(full.shape[0]):
            full[i, pl.ds(at, size), :] = parts[k][first + i]


def split(full, outs, n):
    size = outs[0].shape[1]
    for k in range(n):
        at = pl.multiple_of(owner(k, n) * size, size)
        for i in range(full.shape[0]):
            outs[k][i] = full[i, pl.ds(at, size), :]


def outer_in_kernel(n, owned_c, contract, first, *refs):
    parts, (x, y, placed, full) = refs[:n], refs[n:]
    owned_m, width = full.shape[0], full.shape[2]

    @pl.when(pl.program_id(0) == 0)
    def _():
        assemble(parts, full, n, first)
        for m in range(owned_m):
            hot = place_m(m, owned_m, owned_c, placed.shape[0], width, BF16)
            placed[:, m * width : (m + 1) * width] = dot(hot, full[m], 1, contract).astype(BF16)

    y[...] = dot(placed[...], x[...], 1, 1).astype(BF16)


def outer_in(parts, x, n, owned_c, contract, first, tb):
    tokens, rows = x.shape
    owned_m = parts[0].shape[0] // 2
    width = parts[0].shape[2]
    return pl.pallas_call(
        functools.partial(outer_in_kernel, n, owned_c, contract, first),
        grid=(tokens // tb,),
        in_specs=[VMEM] * n + [pl.BlockSpec((tb, rows), lambda i: (i, 0))],
        out_specs=[pl.BlockSpec((rows, tb), lambda i: (0, i)), pl.BlockSpec((rows, rows), lambda i: (0, 0))],
        out_shape=[jax.ShapeDtypeStruct((rows, tokens), BF16), jax.ShapeDtypeStruct((rows, rows), BF16)],
        scratch_shapes=[pltpu.VMEM((owned_m, width, width), BF16)],
        compiler_params=params(),
        cost_estimate=pl.CostEstimate(flops=2 * tokens * rows * rows, bytes_accessed=4 * tokens * rows, transcendentals=0),
    )(*parts, x)


def outer_out_kernel(n, owned_m, owned_c, *refs):
    v, e, placed, out, *parts = refs[: 4 + n]
    total, full = refs[4 + n :]
    step, width = pl.program_id(0), full.shape[2]

    @pl.when(step == 0)
    def _():
        total[...] = jnp.zeros_like(total)

    out[...] = dot(v[...], placed[...], 0, 0).astype(BF16)
    total[...] += dot(v[...], e[...], 1, 0)

    @pl.when(step == pl.num_programs(0) - 1)
    def _():
        for m in range(owned_m):
            hot = place_m(m, owned_m, owned_c, total.shape[0], width, F32)
            full[m] = dot(hot, total[:, m * width : (m + 1) * width], 0, 0, precision=EXACT)
        split(full, parts, n)


def outer_out(v, e, placed, n, owned_m, owned_c, width, tb):
    tokens, rows = e.shape
    part = jax.ShapeDtypeStruct((owned_m, width // n, width), F32)
    return pl.pallas_call(
        functools.partial(outer_out_kernel, n, owned_m, owned_c),
        grid=(tokens // tb,),
        in_specs=[
            pl.BlockSpec((rows, tb), lambda i: (0, i)),
            pl.BlockSpec((tb, rows), lambda i: (i, 0)),
            pl.BlockSpec((rows, rows), lambda i: (0, 0)),
        ],
        out_specs=[pl.BlockSpec((tb, rows), lambda i: (i, 0))] + [pl.BlockSpec(part.shape, lambda i: (0, 0, 0))] * n,
        out_shape=[jax.ShapeDtypeStruct((tokens, rows), BF16)] + [part] * n,
        scratch_shapes=[pltpu.VMEM((rows, rows), F32), pltpu.VMEM((owned_m, width, width), F32)],
        compiler_params=params(),
        cost_estimate=pl.CostEstimate(flops=4 * tokens * rows * rows, bytes_accessed=6 * tokens * rows, transcendentals=0),
    )(v, e, placed)


def outer_grad_kernel(n, owned_m, owned_c, *refs):
    z, x, *parts = refs[: 2 + n]
    total, full = refs[2 + n :]
    step, width = pl.program_id(0), full.shape[2]

    @pl.when(step == 0)
    def _():
        total[...] = jnp.zeros_like(total)

    total[...] += dot(z[...], x[...], 1, 0)

    @pl.when(step == pl.num_programs(0) - 1)
    def _():
        for m in range(owned_m):
            hot = place_m(m, owned_m, owned_c, total.shape[0], width, F32)
            full[m] = dot(total[:, m * width : (m + 1) * width], hot, 0, 0, precision=EXACT)
        split(full, parts, n)


def outer_grad(z, x, n, owned_m, owned_c, width, tb):
    tokens, rows = x.shape
    part = jax.ShapeDtypeStruct((owned_m, width // n, width), F32)
    return pl.pallas_call(
        functools.partial(outer_grad_kernel, n, owned_m, owned_c),
        grid=(tokens // tb,),
        in_specs=[pl.BlockSpec((rows, tb), lambda i: (0, i)), pl.BlockSpec((tb, rows), lambda i: (i, 0))],
        out_specs=[pl.BlockSpec(part.shape, lambda i: (0, 0, 0))] * n,
        out_shape=[part] * n,
        scratch_shapes=[pltpu.VMEM((rows, rows), F32), pltpu.VMEM((owned_m, width, width), F32)],
        compiler_params=params(),
        cost_estimate=pl.CostEstimate(flops=2 * tokens * rows * rows, bytes_accessed=4 * tokens * rows, transcendentals=0),
    )(z, x)


def inner_fwd_kernel(n, *refs):
    parts2, parts3, (y, v, up2, down3) = refs[:n], refs[n : 2 * n], refs[2 * n : 2 * n + 4]
    full2, full3 = refs[2 * n + 4 :]
    owned_c, nm, pair = full2.shape
    half, rows = pair // 2, y.shape[0]

    @pl.when(pl.program_id(0) == 0)
    def _():
        assemble(parts2, full2, n)
        assemble(parts3, full3, n)
        for c in range(owned_c):
            hot = place_c(c, owned_c, rows, nm, BF16)
            up2[c * pair : (c + 1) * pair, :] = dot(full2[c], hot, 0, 1).astype(BF16)
            down3[:, c * half : (c + 1) * half] = dot(hot, full3[c], 1, 1).astype(BF16)

    block = y[...]
    total = None
    for c in range(owned_c):
        g = dot(up2[c * pair : (c + 1) * pair, :], block, 1, 0)
        gate, up = g[:half], g[half:]
        hidden = (gate * jax.nn.sigmoid(gate) * up).astype(BF16)
        term = dot(down3[:, c * half : (c + 1) * half], hidden, 1, 0)
        total = term if total is None else total + term
    v[...] = total.astype(BF16)


def inner_fwd(parts2, parts3, y, n, tb):
    rows, tokens = y.shape
    owned_c, nm, pair = parts2[0].shape[0], parts2[0].shape[1] * n, parts2[0].shape[2]
    half = pair // 2
    fixed = lambda i: (0, 0)
    return pl.pallas_call(
        functools.partial(inner_fwd_kernel, n),
        grid=(tokens // tb,),
        in_specs=[VMEM] * (2 * n) + [pl.BlockSpec((rows, tb), lambda i: (0, i))],
        out_specs=[
            pl.BlockSpec((rows, tb), lambda i: (0, i)),
            pl.BlockSpec((owned_c * pair, rows), fixed),
            pl.BlockSpec((rows, owned_c * half), fixed),
        ],
        out_shape=[
            jax.ShapeDtypeStruct((rows, tokens), BF16),
            jax.ShapeDtypeStruct((owned_c * pair, rows), BF16),
            jax.ShapeDtypeStruct((rows, owned_c * half), BF16),
        ],
        scratch_shapes=[pltpu.VMEM((owned_c, nm, pair), BF16), pltpu.VMEM((owned_c, half, nm), BF16)],
        compiler_params=params(),
        cost_estimate=pl.CostEstimate(
            flops=6 * tokens * rows * owned_c * half, bytes_accessed=4 * tokens * rows, transcendentals=tokens * owned_c * half
        ),
    )(*parts2, *parts3, y)


def inner_bwd_kernel(n, y, dv, up2, down3, dz, *refs):
    parts2, parts3 = refs[:n], refs[n : 2 * n]
    up3, down2, total2, total3, full2, full3 = refs[2 * n :]
    owned_c, nm, pair = full2.shape
    half, rows = pair // 2, y.shape[0]
    step = pl.program_id(0)

    @pl.when(step == 0)
    def _():
        total2[...] = jnp.zeros_like(total2)
        total3[...] = jnp.zeros_like(total3)
        up3[...] = down3[...].T
        down2[...] = up2[...].T

    block, back = y[...], dv[...]
    total = None
    for c in range(owned_c):
        pairs, halves = slice(c * pair, (c + 1) * pair), slice(c * half, (c + 1) * half)
        g = dot(up2[pairs, :], block, 1, 0)
        gate, up = g[:half], g[half:]
        sigma = jax.nn.sigmoid(gate)
        silu = gate * sigma
        hidden = (silu * up).astype(BF16)
        total3[halves, :] += dot(hidden, back, 1, 1)
        dh = dot(up3[halves, :], back, 1, 0)
        d_gate = (dh * up * (sigma + silu * (1.0 - sigma))).astype(BF16)
        d_up = (dh * silu).astype(BF16)
        dg = jnp.concatenate([d_gate, d_up], axis=0)
        total2[:, pairs] += dot(block, dg, 1, 1)
        term = dot(down2[:, pairs], dg, 1, 0)
        total = term if total is None else total + term
    dz[...] = total.astype(BF16)

    @pl.when(step == pl.num_programs(0) - 1)
    def _():
        for c in range(owned_c):
            hot = place_c(c, owned_c, rows, nm, F32)
            full2[c] = dot(hot, total2[:, c * pair : (c + 1) * pair], 0, 0, precision=EXACT)
            full3[c] = dot(total3[c * half : (c + 1) * half, :], hot, 1, 0, precision=EXACT)
        split(full2, parts2, n)
        split(full3, parts3, n)


def inner_bwd(y, dv, up2, down3, n, nm, owned_c, tb):
    rows, tokens = y.shape
    pair, half = up2.shape[0] // owned_c, down3.shape[1] // owned_c
    part2 = jax.ShapeDtypeStruct((owned_c, nm // n, pair), F32)
    part3 = jax.ShapeDtypeStruct((owned_c, half // n, nm), F32)
    fixed = lambda i: (0, 0)
    fixed3 = lambda i: (0, 0, 0)
    return pl.pallas_call(
        functools.partial(inner_bwd_kernel, n),
        grid=(tokens // tb,),
        in_specs=[
            pl.BlockSpec((rows, tb), lambda i: (0, i)),
            pl.BlockSpec((rows, tb), lambda i: (0, i)),
            pl.BlockSpec(up2.shape, fixed),
            pl.BlockSpec(down3.shape, fixed),
        ],
        out_specs=[pl.BlockSpec((rows, tb), lambda i: (0, i))]
        + [pl.BlockSpec(part2.shape, fixed3)] * n
        + [pl.BlockSpec(part3.shape, fixed3)] * n,
        out_shape=[jax.ShapeDtypeStruct((rows, tokens), BF16)] + [part2] * n + [part3] * n,
        scratch_shapes=[
            pltpu.VMEM((owned_c * half, rows), BF16),
            pltpu.VMEM((rows, owned_c * pair), BF16),
            pltpu.VMEM((rows, owned_c * pair), F32),
            pltpu.VMEM((owned_c * half, rows), F32),
            pltpu.VMEM((owned_c, nm, pair), F32),
            pltpu.VMEM((owned_c, half, nm), F32),
        ],
        compiler_params=params(),
        cost_estimate=pl.CostEstimate(
            flops=16 * tokens * rows * owned_c * half, bytes_accessed=6 * tokens * rows, transcendentals=tokens * owned_c * half
        ),
    )(y, dv, up2, down3)


def finish_kernel(n, *refs):
    parts, (rho, noise, mean_grad, rho_grad) = refs[:n], refs[n:]
    total = parts[0][...]
    for part in parts[1:]:
        total = total + part[...]
    mean_grad[...] = total
    rho_grad[...] = total * noise[...] * jax.nn.sigmoid(rho[...])


def finish(parts, rho, noise):
    n = len(parts)
    return pl.pallas_call(
        functools.partial(finish_kernel, n),
        in_specs=[VMEM] * (n + 2),
        out_specs=[VMEM] * 2,
        out_shape=[jax.ShapeDtypeStruct(rho.shape, F32)] * 2,
        compiler_params=pltpu.CompilerParams(vmem_limit_bytes=50 * 2**20),
    )(*parts, rho, noise)


def shards(
    n,
    tokens,
    cotangent,
    first_mean,
    first_rho,
    first_noise,
    second_mean,
    second_rho,
    second_noise,
    third_mean,
    third_rho,
    third_noise,
    fourth_mean,
    fourth_rho,
    fourth_noise,
):
    owned_m, width = first_mean.shape[0], first_mean.shape[2]
    owned_c, nm = second_mean.shape[0], second_mean.shape[1] * n
    tb = 512

    outer = jnp.concatenate(
        [sampled(first_mean, first_rho, first_noise), sampled(fourth_mean, fourth_rho, fourth_noise)], axis=0
    )
    outer_parts = gather_parts(outer, n)
    y_out, _ = outer_in(outer_parts, tokens, n, owned_c, 1, 0, 1024)
    y = exchange(y_out)
    back_out, placed4 = outer_in(outer_parts, cotangent, n, owned_c, 0, owned_m, 1024)
    back = exchange(back_out)
    parts2 = gather_parts(sampled(second_mean, second_rho, second_noise), n)
    parts3 = gather_parts(sampled(third_mean, third_rho, third_noise), n)
    v_out, up2, down3 = inner_fwd(parts2, parts3, y, n, tb)
    v = exchange(v_out)
    dz_out, *shares = inner_bwd(y, back, up2, down3, n, nm, owned_c, tb)
    dz = exchange(dz_out)
    two = finish(scatter_parts(shares[:n], n), second_rho, second_noise)
    three = finish(scatter_parts(shares[n:], n), third_rho, third_noise)
    layer_out, *share4 = outer_out(v, cotangent, placed4, n, owned_m, owned_c, width, 1024)
    four = finish(scatter_parts(share4, n), fourth_rho, fourth_noise)
    share1 = outer_grad(dz, tokens, n, owned_m, owned_c, width, 1024)
    one = finish(scatter_parts(share1, n), first_rho, first_noise)
    return (layer_out, *one, *two, *three, *four)


def solution(mesh):
    block = P("block", "dp", None)
    rows = P("dp", "block")
    return jax.shard_map(
        functools.partial(shards, mesh.shape["dp"]),
        mesh=mesh,
        in_specs=(rows, rows) + (block,) * 12,
        out_specs=(rows,) + (block,) * 8,
        check_vma=False,
    )
```

time: 311 us -> 179 us (0.58)
  matrix products: 76.8 us -> 0 us
  Pallas kernels: 0 us -> 63.1 us
  local copies, waits for them, and re-layouts: 57.7 us -> 6.91 us
  blocking collectives: 48.9 us -> 0 us
  waiting for transfers between devices: 80.5 us -> 48.6 us
  starting transfers between devices: 26 us -> 57.8 us
  between operations: 14.6 us -> 0.87 us
  other arithmetic: 5.32 us -> 1.09 us
    dot_general x11 -> x0, matrix products: 76.8 us -> none  [the longest x1 21 us: shards(): jnp.einsum('cmt,ckm->ctk', back_three, weight_three, preferred_element_ty...]
    pallas_call x0 -> x10, Pallas kernels: none -> 63.1 us  [the longest x1 27.4 us: inner_bwd(): pl.pallas_call(functools.partial(inner_bwd_kernel, n), grid=(tokens // tb...]
    all_gather x4 -> x0, blocking collectives: 48.9 us -> none  [the longest x1 12.4 us: shards(): lax.all_gather(local_two, 'dp', axis=1, tiled=True)]
    all_to_all x8 -> x0, local copies, waits for them, and re-layouts: 36.1 us -> none  [permute(): lax.all_to_all(blocks, 'block', split_axis=0, concat_axis=1, tiled=True)]
    unnamed x4 -> x0, waiting for transfers between devices: 34 us -> none
    ppermute x0 -> x21, starting transfers between devices: none -> 31.1 us  [the longest x12 15.7 us: scatter_parts(): lax.ppermute(parts[k], 'dp', [(j, (j + k) % n) for j in range(n)])]
    reduce_scatter x2 -> x0, waiting for transfers between devices: 18.9 us -> none  [reduce_share(): return lax.psum_scatter(term, 'dp', scatter_dimension=1, tiled=True)]
    all_to_all x4, waiting for transfers between devices: 27.6 us -> 40.6 us  [exchange(): return lax.all_to_all(x, 'block', split_axis=0, concat_axis=0, tiled=True)]
  transfers between devices with their start and end apart: 7 -> 25, of which waited for: 4 -> 8; matrix products, arithmetic and copies ran while one was open for 18% -> 0% of each run, Pallas kernels for 0% -> 32%
where the time goes in v1:
time: 179 us; the launch traced here: 178 us
  Pallas kernels  63.1 us (35%)
  starting transfers between devices  57.8 us (32%)
  waiting for transfers between devices  48.6 us (27%)
  local copies, waits for them, and re-layouts  6.91 us (4%)
    all_to_all x4, waiting for transfers between devices, exchange(): return lax.all_to_all(x, 'block', split_axis=0, concat_axis=0, tiled=True)  40.6 us
    pallas_call x1, Pallas kernels, inner_bwd(): pl.pallas_call(functools.partial(inner_bwd_kernel, n), grid=(tokens // tb...  27.4 us
    all_to_all x4, starting transfers between devices, exchange(): return lax.all_to_all(x, 'block', split_axis=0, concat_axis=0, tiled=True)  26.7 us
    ppermute x12, starting transfers between devices, scatter_parts(): lax.ppermute(parts[k], 'dp', [(j, (j + k) % n) for j in range(n)])  15.7 us
    ppermute x9, starting transfers between devices, gather_parts(): lax.ppermute(part, 'dp', [(j, (j + k) % n) for j in range(n)])  15.3 us
    pallas_call x1, Pallas kernels, inner_fwd(): pl.pallas_call(functools.partial(inner_fwd_kernel, n), grid=(tokens // tb...  13.6 us
    pallas_call x2, Pallas kernels, outer_in(): pl.pallas_call(functools.partial(outer_in_kernel, n, owned_c, contract, f...  9.27 us
    unnamed x46, local copies, waits for them, and re-layouts  6.91 us
  transfers between devices with their start and end apart: 25, of which 8 were waited for; matrix products, arithmetic and copies ran while one was open for 0% of the time, Pallas kernels for 32%

profile of v1, /device:TPU:0, one launch (start us, length us, event | category | flops | bytes accessed | tf_op | source)
XLA Modules:
  0.0 178.4 jit_solution(7451322948483291111)
XLA Ops:
  1.6 1.6 collective-permute-start.6
  3.2 2.7 %collective-permute-start.7 = (bf16[4,32,128]{2,1,0:T(8,128)(2,1)S(1)}, bf16[4,32,128]{2,1,0:T(8,128)(2,1)S(1)}, u32[]{:S(2)}, u32[]{:S(2)}) collective-permute-start(bf16[4,32,128]{2,1,0:T(8,128)(2,1)S(1)} %pad_maximum_fusion.refs_0_), channel_id=1, source_target_pairs={{0,64},{32,96},{64,0},{96,32},{1,65},{33,97},{65,1},{97,33},{2,66}... | collective-permute-start | bytes 98312 | tf_op jit(solution)/shard_map/ppermute | solution.py:28
  9.8 4.6 %shard_map.205 = (bf16[256,4096]{1,0:T(8,128)(2,1)}, bf16[256,256]{1,0:T(8,128)(2,1)}) custom-call(bf16[4,32,128]{2,1,0:T(8,128)(2,1)S(1)} %pad_maximum_fusion.refs_0_, bf16[4,32,128]{2,1,0:T(8,128)(2,1)S(1)} %collective-permute-done.6.refs_1_, bf16[4,32,128]{2,1,0:T(8,128)(2,1)S(1)} %collective-permute-done.7.refs_2_, ...), custom_call_target="tpu_custom_call" | custom-call | flops 536870912 | bytes 4194304 | tf_op jit(solution)/shard_map/pallas_call | solution.py:92
  14.4 8.5 %all-to-all-start = ((bf16[32,8,4096]{2,1,0:T(8,128)(2,1)}), bf16[32,8,4096]{2,1,0:T(8,128)(2,1)}, u32[]{:S(2)}, u32[]{:S(2)}) async-start(bf16[32,8,4096]{2,1,0:T(8,128)(2,1)} %bitcast), calls=%async_computation | async-start | bytes 4194304 | tf_op jit(solution)/shard_map/all_to_all | solution.py:38
  22.9 4.7 %shard_map.207 = (bf16[256,4096]{1,0:T(8,128)(2,1)}, bf16[256,256]{1,0:T(8,128)(2,1)S(1)}) custom-call(bf16[4,32,128]{2,1,0:T(8,128)(2,1)S(1)} %pad_maximum_fusion.refs_0_, bf16[4,32,128]{2,1,0:T(8,128)(2,1)S(1)} %collective-permute-done.6.refs_1_, bf16[4,32,128]{2,1,0:T(8,128)(2,1)S(1)} %collective-permute-done.7.refs_2_, ...), custom_call_target="tpu_custom_call" | custom-call | flops 536870912 | bytes 4194304 | tf_op jit(solution)/shard_map/pallas_call | solution.py:92
  27.6 25.3 %all-to-all-done = bf16[32,8,4096]{2,1,0:T(8,128)(2,1)} async-done(((bf16[32,8,4096]{2,1,0:T(8,128)(2,1)}), bf16[32,8,4096]{2,1,0:T(8,128)(2,1)}, u32[]{:S(2)}, u32[]{:S(2)}) %all-to-all-start) | async-done | bytes 2097184 | tf_op jit(solution)/shard_map/all_to_all | solution.py:38
  52.9 4.9 %all-to-all-start.2 = ((bf16[32,8,4096]{2,1,0:T(8,128)(2,1)}), bf16[32,8,4096]{2,1,0:T(8,128)(2,1)}, u32[]{:S(2)}, u32[]{:S(2)}) async-start(bf16[32,8,4096]{2,1,0:T(8,128)(2,1)} %bitcast.4), calls=%async_computation.2 | async-start | bytes 4194304 | tf_op jit(solution)/shard_map/all_to_all | solution.py:38
  59.7 3.2 %collective-permute-start.1 = (bf16[4,16,512]{2,1,0:T(8,128)(2,1)S(1)}, bf16[4,16,512]{2,1,0:T(8,128)(2,1)S(1)}, u32[]{:S(2)}, u32[]{:S(2)}) collective-permute-start(bf16[4,16,512]{2,1,0:T(8,128)(2,1)S(1)} %fusion.2.refs_0_), channel_id=1, source_target_pairs={{0,64},{32,96},{64,0},{96,32},{1,65},{33,97},{65,1},{97,33},{2,66}... | collective-permute-start | bytes 196616 | tf_op jit(solution)/shard_map/ppermute | solution.py:28
  62.9 2.0 %collective-permute-start.2 = (bf16[4,16,512]{2,1,0:T(8,128)(2,1)S(1)}, bf16[4,16,512]{2,1,0:T(8,128)(2,1)S(1)}, u32[]{:S(2)}, u32[]{:S(2)}) collective-permute-start(bf16[4,16,512]{2,1,0:T(8,128)(2,1)S(1)} %fusion.2.refs_0_), channel_id=1, source_target_pairs={{0,96},{32,0},{64,32},{96,64},{1,97},{33,1},{65,33},{97,65},{2,98}... | collective-permute-start | bytes 196616 | tf_op jit(solution)/shard_map/ppermute | solution.py:28
  64.9 2.7 %collective-permute-start.5 = (bf16[4,64,64]{2,1,0:T(8,128)(2,1)S(1)}, bf16[4,64,64]{2,1,0:T(8,128)(2,1)S(1)}, u32[]{:S(2)}, u32[]{:S(2)}) collective-permute-start(bf16[4,64,64]{2,1,0:T(8,128)(2,1)S(1)} %fusion.5.refs_4_), channel_id=1, source_target_pairs={{0,96},{32,0},{64,32},{96,64},{1,97},{33,1},{65,33},{97,65},{2,98}... | collective-permute-start | bytes 98312 | tf_op jit(solution)/shard_map/ppermute | solution.py:28
  67.6 3.1 %collective-permute-done.4.refs_6_ = bf16[4,64,64]{2,1,0:T(8,128)(2,1)S(1)} collective-permute-done((bf16[4,64,64]{2,1,0:T(8,128)(2,1)S(1)}, bf16[4,64,64]{2,1,0:T(8,128)(2,1)S(1)}, u32[]{:S(2)}, u32[]{:S(2)}) %collective-permute-start.4) | collective-permute-done | bytes 32800 | tf_op jit(solution)/shard_map/ppermute | solution.py:28
  70.7 13.6 %shard_map.206 = (bf16[256,4096]{1,0:T(8,128)(2,1)}, bf16[2048,256]{1,0:T(8,128)(2,1)S(1)}, bf16[256,1024]{1,0:T(8,128)(2,1)S(1)}) custom-call(bf16[4,16,512]{2,1,0:T(8,128)(2,1)S(1)} %fusion.2.refs_0_, bf16[4,16,512]{2,1,0:T(8,128)(2,1)S(1)} %collective-permute-done.refs_1_, bf16[4,16,512]{2,1,0:T(8,128)(2,1)S(1)} %collective-permute-done.1.refs_2_, ...), custom_call_target="tpu_custom_call" | custom-call | flops 6442450944 | bytes 4194304 | tf_op jit(solution)/shard_map/pallas_call | solution.py:208
  86.2 1.6 all-to-all-done.2
  87.8 6.0 %all-to-all-start.1 = ((bf16[32,8,4096]{2,1,0:T(8,128)(2,1)}), bf16[32,8,4096]{2,1,0:T(8,128)(2,1)S(1)}, u32[]{:S(2)}, u32[]{:S(2)}) async-start(bf16[32,8,4096]{2,1,0:T(8,128)(2,1)} %bitcast.10), calls=%async_computation.1 | async-start | bytes 4194304 | tf_op jit(solution)/shard_map/all_to_all | solution.py:38
  95.0 27.4 %shard_map.209 = (bf16[256,4096]{1,0:T(8,128)(2,1)}, f32[4,16,512]{2,1,0:T(8,128)S(1)}, f32[4,16,512]{2,1,0:T(8,128)S(1)}, f32[4,16,512]{2,1,0:T(8,128)S(1)}, f3...) custom-call(bf16[256,4096]{1,0:T(8,128)(2,1)} %bitcast.1.refs_8_.y, ...), custom_call_target="tpu_custom_call" | custom-call | flops 17179869184 | bytes 6291456 | tf_op jit(solution)/shard_map/pallas_call | solution.py:280
  124.4 7.3 %all-to-all-start.3 = ((bf16[32,8,4096]{2,1,0:T(8,128)(2,1)}), bf16[32,8,4096]{2,1,0:T(8,128)(2,1)}, u32[]{:S(2)}, u32[]{:S(2)}) async-start(bf16[32,8,4096]{2,1,0:T(8,128)(2,1)} %bitcast.9), calls=%async_computation.3 | async-start | bytes 4194304 | tf_op jit(solution)/shard_map/all_to_all | solution.py:38
  132.5 3.2 %collective-permute-start.16 = (f32[4,64,64]{2,1,0:T(8,128)}, f32[4,64,64]{2,1,0:T(8,128)S(1)}, u32[]{:S(2)}, u32[]{:S(2)}) collective-permute-start(f32[4,64,64]{2,1,0:T(8,128)} %get-tuple-element.63), channel_id=1, source_target_pairs={{0,64},{32,96},{64,0},{96,32},{1,65},{33,97},{65,1},{97,33},{2,66}... | collective-permute-start | bytes 196616 | tf_op jit(solution)/shard_map/ppermute | solution.py:33
  139.0 1.8 %collective-permute-start.14 = (f32[4,16,512]{2,1,0:T(8,128)}, f32[4,16,512]{2,1,0:T(8,128)}, u32[]{:S(2)}, u32[]{:S(2)}) collective-permute-start(f32[4,16,512]{2,1,0:T(8,128)} %copy-done.10), channel_id=1, source_target_pairs={{0,96},{32,0},{64,32},{96,64},{1,97},{33,1},{65,33},{97,65},{2,98}... | collective-permute-start | bytes 393224 | tf_op jit(solution)/shard_map/ppermute | solution.py:33
  140.8 5.2 %shard_map.208 = (bf16[4096,256]{1,0:T(8,128)(2,1)}, f32[2,32,128]{2,1,0:T(8,128)S(1)}, f32[2,32,128]{2,1,0:T(8,128)}, f32[2,32,128]{2,1,0:T(8,128)S(1)}, f32[2,32,128]{2,1,0:T(8,128)S(1)}) custom-call(bf16[256,4096]{1,0:T(8,128)(2,1)S(1)} %bitcast.8, bf16[4096,256]{1,0:T(8,128)(2,1)} %refs_1_.2, bf16[256,256]{1,0:T(8,128)(2,1)S(1)} %get-tuple-element.43.refs_2_), custom_call_target="tpu_custom_call" | custom-call | flops 1073741824 | bytes 6291456 | tf_op jit(solution)/shard_map/pallas_call | solution.py:127
  148.0 13.7 %all-to-all-done.3 = bf16[32,8,4096]{2,1,0:T(8,128)(2,1)} async-done(((bf16[32,8,4096]{2,1,0:T(8,128)(2,1)}), bf16[32,8,4096]{2,1,0:T(8,128)(2,1)}, u32[]{:S(2)}, u32[]{:S(2)}) %all-to-all-start.3) | async-done | bytes 2097184 | tf_op jit(solution)/shard_map/all_to_all | solution.py:38
  161.8 4.0 %shard_map.210 = (f32[2,32,128]{2,1,0:T(8,128)S(1)}, f32[2,32,128]{2,1,0:T(8,128)S(1)}, f32[2,32,128]{2,1,0:T(8,128)S(1)}, f32[2,32,128]{2,1,0:T(8,128)S(1)}) custom-call(bf16[256,4096]{1,0:T(8,128)(2,1)} %bitcast.7.refs_0_, bf16[4096,256]{1,0:T(8,128)(2,1)} %refs_1_.3), custom_call_target="tpu_custom_call" | custom-call | flops 536870912 | bytes 4194304 | tf_op jit(solution)/shard_map/pallas_call | solution.py:165
  165.8 2.1 %collective-permute-start.19 = (f32[2,32,128]{2,1,0:T(8,128)S(1)}, f32[2,32,128]{2,1,0:T(8,128)S(1)}, u32[]{:S(2)}, u32[]{:S(2)}) collective-permute-start(f32[2,32,128]{2,1,0:T(8,128)S(1)} %copy-done.16), channel_id=1, source_target_pairs={{0,64},{32,96},{64,0},{96,32},{1,65},{33,97},{65,1},{97,33},{2,66}... | collective-permute-start | bytes 98312 | tf_op jit(solution)/shard_map/ppermute | solution.py:33
  169.2 2.0 %collective-permute-start.10 = (f32[2,32,128]{2,1,0:T(8,128)S(1)}, f32[2,32,128]{2,1,0:T(8,128)S(1)}, u32[]{:S(2)}, u32[]{:S(2)}) collective-permute-start(f32[2,32,128]{2,1,0:T(8,128)S(1)} %get-tuple-element.51), channel_id=1, source_target_pairs={{0,64},{32,96},{64,0},{96,32},{1,65},{33,97},{65,1},{97,33},{2,66}... | collective-permute-start | bytes 98312 | tf_op jit(solution)/shard_map/ppermute | solution.py:33
  173.9 1.7 shard_map.212
  (86 shorter events, 24.6 us)
Async XLA Ops:
  1.6 5.8 %collective-permute-start.6 = (bf16[4,32,128]{2,1,0:T(8,128)(2,1)S(1)}, bf16[4,32,128]{2,1,0:T(8,128)(2,1)S(1)}, u32[]{:S(2)}, u32[]{:S(2)}) collective-permute-start(bf16[4,32,128]{2,1,0:T(8,128)(2,1)S(1)} %pad_maximum_fusion.refs_0_), channel_id=1, source_target_pairs={{0,32},{32,64},{64,96},{96,0},{1,33},{33,65},{65,97},{97,1},{2,34}... | collective-permute-start | bytes 98312 | tf_op jit(solution)/shard_map/ppermute | solution.py:28
  3.2 5.4 %collective-permute-start.7 = (bf16[4,32,128]{2,1,0:T(8,128)(2,1)S(1)}, bf16[4,32,128]{2,1,0:T(8,128)(2,1)S(1)}, u32[]{:S(2)}, u32[]{:S(2)}) collective-permute-start(bf16[4,32,128]{2,1,0:T(8,128)(2,1)S(1)} %pad_maximum_fusion.refs_0_), channel_id=1, source_target_pairs={{0,64},{32,96},{64,0},{96,32},{1,65},{33,97},{65,1},{97,33},{2,66}... | collective-permute-start | bytes 98312 | tf_op jit(solution)/shard_map/ppermute | solution.py:28
  14.4 38.4 %all-to-all-start = ((bf16[32,8,4096]{2,1,0:T(8,128)(2,1)}), bf16[32,8,4096]{2,1,0:T(8,128)(2,1)}, u32[]{:S(2)}, u32[]{:S(2)}) async-start(bf16[32,8,4096]{2,1,0:T(8,128)(2,1)} %bitcast), calls=%async_computation | async-start | bytes 4194304 | tf_op jit(solution)/shard_map/all_to_all | solution.py:38
  52.9 34.9 %all-to-all-start.2 = ((bf16[32,8,4096]{2,1,0:T(8,128)(2,1)}), bf16[32,8,4096]{2,1,0:T(8,128)(2,1)}, u32[]{:S(2)}, u32[]{:S(2)}) async-start(bf16[32,8,4096]{2,1,0:T(8,128)(2,1)} %bitcast.4), calls=%async_computation.2 | async-start | bytes 4194304 | tf_op jit(solution)/shard_map/all_to_all | solution.py:38
  58.0 7.0 %collective-permute-start.3 = (bf16[4,64,64]{2,1,0:T(8,128)(2,1)S(1)}, bf16[4,64,64]{2,1,0:T(8,128)(2,1)S(1)}, u32[]{:S(2)}, u32[]{:S(2)}) collective-permute-start(bf16[4,64,64]{2,1,0:T(8,128)(2,1)S(1)} %fusion.5.refs_4_), channel_id=1, source_target_pairs={{0,32},{32,64},{64,96},{96,0},{1,33},{33,65},{65,97},{97,1},{2,34}... | collective-permute-start | bytes 98312 | tf_op jit(solution)/shard_map/ppermute | solution.py:28
  58.4 12.3 %collective-permute-start = (bf16[4,16,512]{2,1,0:T(8,128)(2,1)S(1)}, bf16[4,16,512]{2,1,0:T(8,128)(2,1)S(1)}, u32[]{:S(2)}, u32[]{:S(2)}) collective-permute-start(bf16[4,16,512]{2,1,0:T(8,128)(2,1)S(1)} %fusion.2.refs_0_), channel_id=1, source_target_pairs={{0,32},{32,64},{64,96},{96,0},{1,33},{33,65},{65,97},{97,1},{2,34}... | collective-permute-start | bytes 196616 | tf_op jit(solution)/shard_map/ppermute | solution.py:28
  59.7 11.1 %collective-permute-start.1 = (bf16[4,16,512]{2,1,0:T(8,128)(2,1)S(1)}, bf16[4,16,512]{2,1,0:T(8,128)(2,1)S(1)}, u32[]{:S(2)}, u32[]{:S(2)}) collective-permute-start(bf16[4,16,512]{2,1,0:T(8,128)(2,1)S(1)} %fusion.2.refs_0_), channel_id=1, source_target_pairs={{0,64},{32,96},{64,0},{96,32},{1,65},{33,97},{65,1},{97,33},{2,66}... | collective-permute-start | bytes 196616 | tf_op jit(solution)/shard_map/ppermute | solution.py:28
  62.9 7.8 %collective-permute-start.2 = (bf16[4,16,512]{2,1,0:T(8,128)(2,1)S(1)}, bf16[4,16,512]{2,1,0:T(8,128)(2,1)S(1)}, u32[]{:S(2)}, u32[]{:S(2)}) collective-permute-start(bf16[4,16,512]{2,1,0:T(8,128)(2,1)S(1)} %fusion.2.refs_0_), channel_id=1, source_target_pairs={{0,96},{32,0},{64,32},{96,64},{1,97},{33,1},{65,33},{97,65},{2,98}... | collective-permute-start | bytes 196616 | tf_op jit(solution)/shard_map/ppermute | solution.py:28
  64.9 5.8 %collective-permute-start.4 = (bf16[4,64,64]{2,1,0:T(8,128)(2,1)S(1)}, bf16[4,64,64]{2,1,0:T(8,128)(2,1)S(1)}, u32[]{:S(2)}, u32[]{:S(2)}) collective-permute-start(bf16[4,64,64]{2,1,0:T(8,128)(2,1)S(1)} %fusion.5.refs_4_), channel_id=1, source_target_pairs={{0,64},{32,96},{64,0},{96,32},{1,65},{33,97},{65,1},{97,33},{2,66}... | collective-permute-start | bytes 98312 | tf_op jit(solution)/shard_map/ppermute | solution.py:28
  64.9 5.8 %collective-permute-start.5 = (bf16[4,64,64]{2,1,0:T(8,128)(2,1)S(1)}, bf16[4,64,64]{2,1,0:T(8,128)(2,1)S(1)}, u32[]{:S(2)}, u32[]{:S(2)}) collective-permute-start(bf16[4,64,64]{2,1,0:T(8,128)(2,1)S(1)} %fusion.5.refs_4_), channel_id=1, source_target_pairs={{0,96},{32,0},{64,32},{96,64},{1,97},{33,1},{65,33},{97,65},{2,98}... | collective-permute-start | bytes 98312 | tf_op jit(solution)/shard_map/ppermute | solution.py:28
  87.8 36.6 %all-to-all-start.1 = ((bf16[32,8,4096]{2,1,0:T(8,128)(2,1)}), bf16[32,8,4096]{2,1,0:T(8,128)(2,1)S(1)}, u32[]{:S(2)}, u32[]{:S(2)}) async-start(bf16[32,8,4096]{2,1,0:T(8,128)(2,1)} %bitcast.10), calls=%async_computation.1 | async-start | bytes 4194304 | tf_op jit(solution)/shard_map/all_to_all | solution.py:38
  124.4 37.3 %all-to-all-start.3 = ((bf16[32,8,4096]{2,1,0:T(8,128)(2,1)}), bf16[32,8,4096]{2,1,0:T(8,128)(2,1)}, u32[]{:S(2)}, u32[]{:S(2)}) async-start(bf16[32,8,4096]{2,1,0:T(8,128)(2,1)} %bitcast.9), calls=%async_computation.3 | async-start | bytes 4194304 | tf_op jit(solution)/shard_map/all_to_all | solution.py:38
  131.8 7.2 %collective-permute-start.15 = (f32[4,64,64]{2,1,0:T(8,128)}, f32[4,64,64]{2,1,0:T(8,128)S(1)}, u32[]{:S(2)}, u32[]{:S(2)}) collective-permute-start(f32[4,64,64]{2,1,0:T(8,128)} %get-tuple-element.62), channel_id=1, source_target_pairs={{0,32},{32,64},{64,96},{96,0},{1,33},{33,65},{65,97},{97,1},{2,34}... | collective-permute-start | bytes 196616 | tf_op jit(solution)/shard_map/ppermute | solution.py:33
  132.5 15.3 %collective-permute-start.16 = (f32[4,64,64]{2,1,0:T(8,128)}, f32[4,64,64]{2,1,0:T(8,128)S(1)}, u32[]{:S(2)}, u32[]{:S(2)}) collective-permute-start(f32[4,64,64]{2,1,0:T(8,128)} %get-tuple-element.63), channel_id=1, source_target_pairs={{0,64},{32,96},{64,0},{96,32},{1,65},{33,97},{65,1},{97,33},{2,66}... | collective-permute-start | bytes 196616 | tf_op jit(solution)/shard_map/ppermute | solution.py:33
  135.7 30.1 %collective-permute-start.17 = (f32[4,64,64]{2,1,0:T(8,128)}, f32[4,64,64]{2,1,0:T(8,128)S(1)}, u32[]{:S(2)}, u32[]{:S(2)}) collective-permute-start(f32[4,64,64]{2,1,0:T(8,128)} %get-tuple-element.64), channel_id=1, source_target_pairs={{0,96},{32,0},{64,32},{96,64},{1,97},{33,1},{65,33},{97,65},{2,98}... | collective-permute-start | bytes 196616 | tf_op jit(solution)/shard_map/ppermute | solution.py:33
  136.5 31.4 %collective-permute-start.12 = (f32[4,16,512]{2,1,0:T(8,128)}, f32[4,16,512]{2,1,0:T(8,128)S(1)}, u32[]{:S(2)}, u32[]{:S(2)}) collective-permute-start(f32[4,16,512]{2,1,0:T(8,128)} %copy-done.12), channel_id=1, source_target_pairs={{0,32},{32,64},{64,96},{96,0},{1,33},{33,65},{65,97},{97,1},{2,34}... | collective-permute-start | bytes 393224 | tf_op jit(solution)/shard_map/ppermute | solution.py:33
  137.7 31.5 %collective-permute-start.13 = (f32[4,16,512]{2,1,0:T(8,128)}, f32[4,16,512]{2,1,0:T(8,128)}, u32[]{:S(2)}, u32[]{:S(2)}) collective-permute-start(f32[4,16,512]{2,1,0:T(8,128)} %copy-done.11), channel_id=1, source_target_pairs={{0,64},{32,96},{64,0},{96,32},{1,65},{33,97},{65,1},{97,33},{2,66}... | collective-permute-start | bytes 393224 | tf_op jit(solution)/shard_map/ppermute | solution.py:33
  139.0 32.2 %collective-permute-start.14 = (f32[4,16,512]{2,1,0:T(8,128)}, f32[4,16,512]{2,1,0:T(8,128)}, u32[]{:S(2)}, u32[]{:S(2)}) collective-permute-start(f32[4,16,512]{2,1,0:T(8,128)} %copy-done.10), channel_id=1, source_target_pairs={{0,96},{32,0},{64,32},{96,64},{1,97},{33,1},{65,33},{97,65},{2,98}... | collective-permute-start | bytes 393224 | tf_op jit(solution)/shard_map/ppermute | solution.py:33
  147.8 24.8 %collective-permute-start.18 = (f32[2,32,128]{2,1,0:T(8,128)}, f32[2,32,128]{2,1,0:T(8,128)S(1)}, u32[]{:S(2)}, u32[]{:S(2)}) collective-permute-start(f32[2,32,128]{2,1,0:T(8,128)} %get-tuple-element.68), channel_id=1, source_target_pairs={{0,32},{32,64},{64,96},{96,0},{1,33},{33,65},{65,97},{97,1},{2,34}... | collective-permute-start | bytes 98312 | tf_op jit(solution)/shard_map/ppermute | solution.py:33
  165.8 9.9 %collective-permute-start.19 = (f32[2,32,128]{2,1,0:T(8,128)S(1)}, f32[2,32,128]{2,1,0:T(8,128)S(1)}, u32[]{:S(2)}, u32[]{:S(2)}) collective-permute-start(f32[2,32,128]{2,1,0:T(8,128)S(1)} %copy-done.16), channel_id=1, source_target_pairs={{0,64},{32,96},{64,0},{96,32},{1,65},{33,97},{65,1},{97,33},{2,66}... | collective-permute-start | bytes 98312 | tf_op jit(solution)/shard_map/ppermute | solution.py:33
  167.9 7.8 %collective-permute-start.20 = (f32[2,32,128]{2,1,0:T(8,128)S(1)}, f32[2,32,128]{2,1,0:T(8,128)S(1)}, u32[]{:S(2)}, u32[]{:S(2)}) collective-permute-start(f32[2,32,128]{2,1,0:T(8,128)S(1)} %copy-done.14), channel_id=1, source_target_pairs={{0,96},{32,0},{64,32},{96,64},{1,97},{33,1},{65,33},{97,65},{2,98}... | collective-permute-start | bytes 98312 | tf_op jit(solution)/shard_map/ppermute | solution.py:33
  169.2 7.1 %collective-permute-start.10 = (f32[2,32,128]{2,1,0:T(8,128)S(1)}, f32[2,32,128]{2,1,0:T(8,128)S(1)}, u32[]{:S(2)}, u32[]{:S(2)}) collective-permute-start(f32[2,32,128]{2,1,0:T(8,128)S(1)} %get-tuple-element.51), channel_id=1, source_target_pairs={{0,64},{32,96},{64,0},{96,32},{1,65},{33,97},{65,1},{97,33},{2,66}... | collective-permute-start | bytes 98312 | tf_op jit(solution)/shard_map/ppermute | solution.py:33
  171.2 5.1 %collective-permute-start.11 = (f32[2,32,128]{2,1,0:T(8,128)S(1)}, f32[2,32,128]{2,1,0:T(8,128)S(1)}, u32[]{:S(2)}, u32[]{:S(2)}) collective-permute-start(f32[2,32,128]{2,1,0:T(8,128)S(1)} %get-tuple-element.52), channel_id=1, source_target_pairs={{0,96},{32,0},{64,32},{96,64},{1,97},{33,1},{65,33},{97,65},{2,98}... | collective-permute-start | bytes 98312 | tf_op jit(solution)/shard_map/ppermute | solution.py:33
  172.6 5.1 %collective-permute-start.9 = (f32[2,32,128]{2,1,0:T(8,128)S(1)}, f32[2,32,128]{2,1,0:T(8,128)S(1)}, u32[]{:S(2)}, u32[]{:S(2)}) collective-permute-start(f32[2,32,128]{2,1,0:T(8,128)S(1)} %get-tuple-element.50), channel_id=1, source_target_pairs={{0,32},{32,64},{64,96},{96,0},{1,33},{33,65},{65,97},{97,1},{2,34}... | collective-permute-start | bytes 98312 | tf_op jit(solution)/shard_map/ppermute | solution.py:33
  (24 other events, 131.7 us)

commit v2 on v1

v2 whole, which is shorter than its diff:
```python
import functools

import jax
import jax.numpy as jnp
from jax import lax
from jax.experimental import pallas as pl
from jax.experimental.pallas import tpu as pltpu
from jax.sharding import PartitionSpec as P

F32, BF16 = jnp.float32, jnp.bfloat16
VMEM = pl.BlockSpec(memory_space=pltpu.VMEM)
HBM = pl.BlockSpec(memory_space=pltpu.HBM)
LANES = 128


def dot(a, b, ca, cb, **kw):
    return lax.dot_general(a, b, (((ca,), (cb,)), ((), ())), preferred_element_type=F32, **kw)


def picked(a, b, ca, cb):
    total = None
    first = a.dtype == BF16
    rest = b if first else a
    for _ in range(3):
        part = rest.astype(BF16)
        rest = rest - part.astype(F32)
        term = dot(a, part, ca, cb) if first else dot(part, b, ca, cb)
        total = term if total is None else total + term
    return total


def logistic(v):
    return 0.5 * jnp.tanh(0.5 * v) + 0.5


def sampled(mean, rho, noise):
    return (mean + jax.nn.softplus(rho) * noise).astype(BF16)


def params(mib):
    return pltpu.CompilerParams(vmem_limit_bytes=mib * 2**20, dimension_semantics=("arbitrary",))


def gather_parts(part, n):
    return [part] + [lax.ppermute(part, "dp", [(j, (j + k) % n) for j in range(n)]) for k in range(1, n)]


def scatter_parts(parts, n):
    return [parts[0]] + [
        lax.ppermute(parts[k], "dp", [(j, (j + k) % n) for j in range(n)]) for k in range(1, n)
    ]


def exchange(x):
    return lax.all_to_all(x, "block", split_axis=0, concat_axis=0, tiled=True)


def place_m(m, owned_m, owned_c, rows, width, dtype):
    r = lax.broadcasted_iota(jnp.int32, (rows, width), 0)
    c = lax.broadcasted_iota(jnp.int32, (rows, width), 1)
    hit = (r // owned_c % owned_m == m) & (r // (owned_m * owned_c) * owned_c + r % owned_c == c)
    return jnp.where(hit, 1.0, 0.0).astype(dtype)


def place_c(c, owned_c, rows, width, dtype):
    r = lax.broadcasted_iota(jnp.int32, (rows, width), 0)
    m = lax.broadcasted_iota(jnp.int32, (rows, width), 1)
    return jnp.where((r % owned_c == c) & (r // owned_c == m), 1.0, 0.0).astype(dtype)


def owner(k, n):
    return lax.rem(lax.axis_index("dp") + (n + k), n)


def assemble(parts, full, n, first=0):
    size = parts[0].shape[1]
    for k in range(n):
        at = pl.multiple_of(owner(-k, n) * size, size)
        for i in range(full.shape[0]):
            full[i, pl.ds(at, size), :] = parts[k][first + i]


def split(full, outs, n):
    size = outs[0].shape[1]
    for k in range(n):
        at = pl.multiple_of(owner(k, n) * size, size)
        for i in range(full.shape[0]):
            outs[k][i] = full[i, pl.ds(at, size), :]


def chunks(total, count):
    size = total // count
    return [slice(k * size, (k + 1) * size) for k in range(count)]


def stash_kernel(count, x, *refs):
    held, done = refs[-2:]
    copies = [
        pltpu.make_async_copy(x.at[rows], held.at[rows], done.at[k]) for k, rows in enumerate(chunks(x.shape[0], count))
    ]
    for copy in copies:
        copy.start()
    for copy in copies:
        copy.wait()


def stash(x, after=()):
    count = 4
    return pl.pallas_call(
        functools.partial(stash_kernel, count),
        in_specs=[HBM] * (1 + len(after)),
        out_specs=VMEM,
        out_shape=pltpu.VMEM(x.shape, x.dtype),
        scratch_shapes=[pltpu.SemaphoreType.DMA((count,))],
        compiler_params=pltpu.CompilerParams(vmem_limit_bytes=16 * 2**20),
        cost_estimate=pl.CostEstimate(flops=0, bytes_accessed=4 * x.size, transcendentals=0),
    )(x, *after)


def outer_in_kernel(n, owned_c, contract, first, count, *refs):
    parts, x = refs[:n], refs[n]
    y, placed, full, held, done = refs[-5:]
    owned_m, width = full.shape[0], full.shape[2]
    assemble(parts, full, n, first)
    for m in range(owned_m):
        hot = place_m(m, owned_m, owned_c, placed.shape[0], width, BF16)
        placed[:, m * width : (m + 1) * width] = dot(hot, full[m], 1, contract).astype(BF16)
    copies = []
    for k, cols in enumerate(chunks(x.shape[0], count)):
        held[:, cols] = dot(placed[...], x[cols, :], 1, 1).astype(BF16)
        copies.append(pltpu.make_async_copy(held.at[:, cols], y.at[:, cols], done.at[k]))
        copies[k].start()
    for copy in copies:
        copy.wait()


def outer_in(parts, x, n, owned_c, contract, first, after=()):
    tokens, rows = x.shape
    owned_m, width = parts[0].shape[0] // 2, parts[0].shape[2]
    count = 4
    return pl.pallas_call(
        functools.partial(outer_in_kernel, n, owned_c, contract, first, count),
        in_specs=[VMEM] * (n + 1) + [HBM] * len(after),
        out_specs=[HBM, VMEM],
        out_shape=[pltpu.HBM((rows, tokens), BF16), jax.ShapeDtypeStruct((rows, rows), BF16)],
        scratch_shapes=[
            pltpu.VMEM((owned_m, width, width), BF16),
            pltpu.VMEM((rows, tokens), BF16),
            pltpu.SemaphoreType.DMA((count,)),
        ],
        compiler_params=pltpu.CompilerParams(vmem_limit_bytes=24 * 2**20),
        cost_estimate=pl.CostEstimate(flops=2 * tokens * rows * rows, bytes_accessed=4 * tokens * rows, transcendentals=0),
    )(*parts, x, *after)


def outer_out_kernel(n, owned_m, owned_c, *refs):
    v, e, placed, out, *parts = refs[: 4 + n]
    total, full = refs[4 + n :]
    step, width = pl.program_id(0), full.shape[2]

    @pl.when(step == 0)
    def _():
        total[...] = jnp.zeros_like(total)

    out[...] = dot(v[...], placed[...], 0, 0).astype(BF16)
    total[...] += dot(v[...], e[...], 1, 0)

    @pl.when(step == pl.num_programs(0) - 1)
    def _():
        for m in range(owned_m):
            hot = place_m(m, owned_m, owned_c, total.shape[0], width, BF16)
            full[m] = picked(hot, total[:, m * width : (m + 1) * width], 0, 0)
        split(full, parts, n)


def outer_out(v, e, placed, n, owned_m, owned_c, width, tb):
    tokens, rows = e.shape
    part = jax.ShapeDtypeStruct((owned_m, width // n, width), F32)
    return pl.pallas_call(
        functools.partial(outer_out_kernel, n, owned_m, owned_c),
        grid=(tokens // tb,),
        in_specs=[
            pl.BlockSpec((rows, tb), lambda i: (0, i)),
            pl.BlockSpec((tb, rows), lambda i: (i, 0)),
            pl.BlockSpec((rows, rows), lambda i: (0, 0)),
        ],
        out_specs=[pl.BlockSpec((tb, rows), lambda i: (i, 0))] + [pl.BlockSpec(part.shape, lambda i: (0, 0, 0))] * n,
        out_shape=[jax.ShapeDtypeStruct((tokens, rows), BF16)] + [part] * n,
        scratch_shapes=[pltpu.VMEM((rows, rows), F32), pltpu.VMEM((owned_m, width, width), F32)],
        compiler_params=params(24),
        cost_estimate=pl.CostEstimate(flops=4 * tokens * rows * rows, bytes_accessed=6 * tokens * rows, transcendentals=0),
    )(v, e, placed)


def outer_grad_kernel(n, owned_m, owned_c, count, *refs):
    z, x = refs[:2]
    *parts, held, full, done = refs[-n - 3 :]
    width = full.shape[2]
    pieces = chunks(x.shape[0], count)
    copies = [pltpu.make_async_copy(z.at[:, cols], held.at[:, cols], done.at[k]) for k, cols in enumerate(pieces)]
    for copy in copies:
        copy.start()
    total = None
    for copy, cols in zip(copies, pieces):
        copy.wait()
        term = dot(held[:, cols], x[cols, :], 1, 0)
        total = term if total is None else total + term
    for m in range(owned_m):
        hot = place_m(m, owned_m, owned_c, total.shape[0], width, BF16)
        full[m] = picked(total[:, m * width : (m + 1) * width], hot, 0, 0)
    split(full, parts, n)


def outer_grad(z, x, n, owned_m, owned_c, width):
    tokens, rows = x.shape
    count = 4
    part = jax.ShapeDtypeStruct((owned_m, width // n, width), F32)
    return pl.pallas_call(
        functools.partial(outer_grad_kernel, n, owned_m, owned_c, count),
        in_specs=[HBM, VMEM],
        out_specs=[VMEM] * n,
        out_shape=[part] * n,
        scratch_shapes=[
            pltpu.VMEM((rows, tokens), BF16),
            pltpu.VMEM((owned_m, width, width), F32),
            pltpu.SemaphoreType.DMA((count,)),
        ],
        compiler_params=pltpu.CompilerParams(vmem_limit_bytes=24 * 2**20),
        cost_estimate=pl.CostEstimate(flops=2 * tokens * rows * rows, bytes_accessed=4 * tokens * rows, transcendentals=0),
    )(z, x)


def pack_shape(owned_c, own2, pair, own3, nm):
    assert own2 * (pair // LANES) == own3 and 2 * nm == LANES and owned_c % 2 == 0
    return (owned_c + owned_c // 2, own3, LANES)


def each_piece2(owned_c, own2, pair):
    for c in range(owned_c):
        for piece in range(pair // LANES):
            yield c, slice(piece * own2, (piece + 1) * own2), slice(piece * LANES, (piece + 1) * LANES)


def each_piece3(owned_c, nm):
    for c in range(owned_c):
        yield c, owned_c + c // 2, slice(c % 2 * nm, (c % 2 + 1) * nm)


def sample_kernel(mean2, rho2, noise2, mean3, rho3, noise3, *refs):
    packed = refs[-1]
    owned_c, own2, pair = mean2.shape
    for c, rows, cols in each_piece2(owned_c, own2, pair):
        packed[c, rows, :] = sampled(mean2[c, :, cols], rho2[c, :, cols], noise2[c, :, cols])
    for c, at, cols in each_piece3(owned_c, mean3.shape[2]):
        packed[at, :, cols] = sampled(mean3[c], rho3[c], noise3[c])


def sample_inner(second, third, after=()):
    shape = pack_shape(*second[0].shape, *third[0].shape[1:])
    return pl.pallas_call(
        sample_kernel,
        in_specs=[VMEM] * 6 + [HBM] * len(after),
        out_specs=VMEM,
        out_shape=jax.ShapeDtypeStruct(shape, BF16),
        compiler_params=pltpu.CompilerParams(vmem_limit_bytes=16 * 2**20),
    )(*second, *third, *after)


def inner_fwd_kernel(n, *refs):
    parts, (y, v, up2, down3) = refs[:n], refs[n : n + 4]
    full2, full3 = refs[n + 4 :]
    owned_c, nm, pair = full2.shape
    half, rows = pair // 2, y.shape[0]
    own2, own3 = nm // n, half // n

    @pl.when(pl.program_id(0) == 0)
    def _():
        for k in range(n):
            at2 = pl.multiple_of(owner(-k, n) * own2, own2)
            at3 = pl.multiple_of(owner(-k, n) * own3, own3)
            for c, piece, cols in each_piece2(owned_c, own2, pair):
                full2[c, pl.ds(at2, own2), cols] = parts[k][c, piece, :]
            for c, at, cols in each_piece3(owned_c, nm):
                full3[c, pl.ds(at3, own3), :] = parts[k][at, :, cols]
        for c in range(owned_c):
            hot = place_c(c, owned_c, rows, nm, BF16)
            up2[c * pair : (c + 1) * pair, :] = dot(full2[c], hot, 0, 1).astype(BF16)
            down3[:, c * half : (c + 1) * half] = dot(hot, full3[c], 1, 1).astype(BF16)

    block = y[...]
    total = None
    for c in range(owned_c):
        g = dot(up2[c * pair : (c + 1) * pair, :], block, 1, 0)
        gate, up = g[:half], g[half:]
        hidden = (gate * logistic(gate) * up).astype(BF16)
        term = dot(down3[:, c * half : (c + 1) * half], hidden, 1, 0)
        total = term if total is None else total + term
    v[...] = total.astype(BF16)


def inner_fwd(parts, y, n, owned_c, nm, half, tb):
    rows, tokens = y.shape
    pair = 2 * half
    fixed = lambda i: (0, 0)
    return pl.pallas_call(
        functools.partial(inner_fwd_kernel, n),
        grid=(tokens // tb,),
        in_specs=[VMEM] * n + [pl.BlockSpec((rows, tb), lambda i: (0, i))],
        out_specs=[
            pl.BlockSpec((rows, tb), lambda i: (0, i)),
            pl.BlockSpec((owned_c * pair, rows), fixed),
            pl.BlockSpec((rows, owned_c * half), fixed),
        ],
        out_shape=[
            pltpu.HBM((rows, tokens), BF16),
            pltpu.HBM((owned_c * pair, rows), BF16),
            pltpu.HBM((rows, owned_c * half), BF16),
        ],
        scratch_shapes=[pltpu.VMEM((owned_c, nm, pair), BF16), pltpu.VMEM((owned_c, half, nm), BF16)],
        compiler_params=params(32),
        cost_estimate=pl.CostEstimate(
            flops=6 * tokens * rows * owned_c * half, bytes_accessed=4 * tokens * rows, transcendentals=tokens * owned_c * half
        ),
    )(*parts, y)


def inner_bwd_kernel(n, owned_c, y, dv, up2, down3, dz, *refs):
    parts, (up3, down2, total2, total3) = refs[:n], refs[n:]
    rows = y.shape[0]
    nm, pair = rows // owned_c, up2.shape[0] // owned_c
    half = pair // 2
    own2, own3 = nm // n, half // n
    step = pl.program_id(0)

    @pl.when(step == 0)
    def _():
        total2[...] = jnp.zeros_like(total2)
        total3[...] = jnp.zeros_like(total3)
        up3[...] = down3[...].T
        down2[...] = up2[...].T

    block, back = y[...], dv[...]
    back_t = back.T
    total = None
    for c in range(owned_c):
        pairs, halves = slice(c * pair, (c + 1) * pair), slice(c * half, (c + 1) * half)
        g = dot(up2[pairs, :], block, 1, 0)
        gate, up = g[:half], g[half:]
        sigma = logistic(gate)
        silu = gate * sigma
        hidden = (silu * up).astype(BF16)
        total3[halves, :] += dot(hidden, back_t, 1, 0)
        dh = dot(up3[halves, :], back, 1, 0)
        d_gate = (dh * up * (sigma + silu * (1.0 - sigma))).astype(BF16)
        d_up = (dh * silu).astype(BF16)
        dg = jnp.concatenate([d_gate, d_up], axis=0)
        both = dot(block, dg, 1, 1)
        for piece in range(pair // LANES):
            total2[c * (pair // LANES) + piece] += both[:, piece * LANES : (piece + 1) * LANES]
        term = dot(down2[:, pairs], dg, 1, 0)
        total = term if total is None else total + term
    dz[...] = total.astype(BF16)

    @pl.when(step == pl.num_programs(0) - 1)
    def _():
        for k in range(n):
            at2 = owner(k, n) * (own2 * owned_c)
            for c, piece, cols in each_piece2(owned_c, own2, pair):
                held = total2.at[(c * pair + cols.start) // LANES]
                parts[k][c, piece, :] = held[pl.ds(at2 + c, own2, stride=owned_c), :]
        for c, at, cols in each_piece3(owned_c, nm):
            hot = place_c(c, owned_c, rows, nm, BF16)
            for k in range(n):
                at3 = pl.multiple_of(c * half + owner(k, n) * own3, own3)
                parts[k][at, :, cols] = picked(total3[pl.ds(at3, own3), :], hot, 1, 0)


def inner_bwd(y, dv, up2, down3, n, owned_c, tb):
    rows, tokens = y.shape
    pair, half, nm = up2.shape[0] // owned_c, down3.shape[1] // owned_c, rows // owned_c
    part = jax.ShapeDtypeStruct(pack_shape(owned_c, nm // n, pair, half // n, nm), F32)
    fixed = lambda i: (0, 0)
    fixed3 = lambda i: (0, 0, 0)
    return pl.pallas_call(
        functools.partial(inner_bwd_kernel, n, owned_c),
        grid=(tokens // tb,),
        in_specs=[
            pl.BlockSpec((rows, tb), lambda i: (0, i)),
            pl.BlockSpec((rows, tb), lambda i: (0, i)),
            pl.BlockSpec(up2.shape, fixed),
            pl.BlockSpec(down3.shape, fixed),
        ],
        out_specs=[pl.BlockSpec((rows, tb), lambda i: (0, i))] + [pl.BlockSpec(part.shape, fixed3)] * n,
        out_shape=[pltpu.HBM((rows, tokens), BF16)] + [pltpu.HBM(part.shape, part.dtype)] * n,
        scratch_shapes=[
            pltpu.VMEM((owned_c * half, rows), BF16),
            pltpu.VMEM((rows, owned_c * pair), BF16),
            pltpu.VMEM((owned_c * pair // LANES, rows, LANES), F32),
            pltpu.VMEM((owned_c * half, rows), F32),
        ],
        compiler_params=params(32),
        cost_estimate=pl.CostEstimate(
            flops=16 * tokens * rows * owned_c * half, bytes_accessed=6 * tokens * rows, transcendentals=tokens * owned_c * half
        ),
    )(y, dv, *(pltpu.with_memory_space_constraint(w, pltpu.HBM) for w in (up2, down3)))


def added(parts):
    total = parts[0]
    for part in parts[1:]:
        total = total + part
    return total


def finish_inner_kernel(n, *refs):
    parts, (rho2, noise2, rho3, noise3, mean2, grad2, mean3, grad3) = refs[:n], refs[n:]
    owned_c, own2, pair = rho2.shape
    for c, rows, cols in each_piece2(owned_c, own2, pair):
        total = added([part[c, rows, :] for part in parts])
        mean2[c, :, cols] = total
        grad2[c, :, cols] = total * noise2[c, :, cols] * logistic(rho2[c, :, cols])
    for c, at, cols in each_piece3(owned_c, rho3.shape[2]):
        total = added([part[at, :, cols] for part in parts])
        mean3[c] = total
        grad3[c] = total * noise3[c] * logistic(rho3[c])


def finish_inner(parts, rho2, noise2, rho3, noise3):
    n = len(parts)
    return pl.pallas_call(
        functools.partial(finish_inner_kernel, n),
        in_specs=[VMEM] * (n + 4),
        out_specs=[VMEM] * 4,
        out_shape=[jax.ShapeDtypeStruct(rho2.shape, F32)] * 2 + [jax.ShapeDtypeStruct(rho3.shape, F32)] * 2,
        compiler_params=pltpu.CompilerParams(vmem_limit_bytes=16 * 2**20),
    )(*parts, rho2, noise2, rho3, noise3)


def finish_kernel(n, *refs):
    parts, (rho, noise, mean_grad, rho_grad) = refs[:n], refs[n:]
    total = added([part[...] for part in parts])
    mean_grad[...] = total
    rho_grad[...] = total * noise[...] * logistic(rho[...])


def finish(parts, rho, noise):
    n = len(parts)
    return pl.pallas_call(
        functools.partial(finish_kernel, n),
        in_specs=[VMEM] * (n + 2),
        out_specs=[VMEM] * 2,
        out_shape=[jax.ShapeDtypeStruct(rho.shape, F32)] * 2,
        compiler_params=pltpu.CompilerParams(vmem_limit_bytes=16 * 2**20),
    )(*parts, rho, noise)


def shards(
    n,
    tokens,
    cotangent,
    first_mean,
    first_rho,
    first_noise,
    second_mean,
    second_rho,
    second_noise,
    third_mean,
    third_rho,
    third_noise,
    fourth_mean,
    fourth_rho,
    fourth_noise,
):
    owned_m, width = first_mean.shape[0], first_mean.shape[2]
    owned_c, nm = second_mean.shape[0], second_mean.shape[1] * n
    half = third_mean.shape[1] * n

    outer = jnp.concatenate(
        [sampled(first_mean, first_rho, first_noise), sampled(fourth_mean, fourth_rho, fourth_noise)], axis=0
    )
    outer_parts = gather_parts(outer, n)
    y_out, placed1 = outer_in(outer_parts, stash(tokens), n, owned_c, 1, 0)
    y = exchange(y_out)
    inner = sample_inner((second_mean, second_rho, second_noise), (third_mean, third_rho, third_noise), (placed1,))
    inner_parts = gather_parts(inner, n)
    back_out, placed4 = outer_in(outer_parts, cotangent, n, owned_c, 0, owned_m, inner_parts)
    back = exchange(back_out)
    v_out, up2, down3 = inner_fwd(inner_parts, y, n, owned_c, nm, half, 1024)
    v = exchange(v_out)
    dz_out, *shares = inner_bwd(y, back, up2, down3, n, owned_c, 1024)
    dz = exchange(dz_out)
    two_three = finish_inner(scatter_parts(shares, n), second_rho, second_noise, third_rho, third_noise)
    layer_out, *share4 = outer_out(v, cotangent, placed4, n, owned_m, owned_c, width, 2048)
    four = finish(scatter_parts(share4, n), fourth_rho, fourth_noise)
    share1 = outer_grad(dz, stash(tokens, (two_three[0], four[0])), n, owned_m, owned_c, width)
    one = finish(scatter_parts(share1, n), first_rho, first_noise)
    return (layer_out, *one, *two_three, *four)


def solution(mesh):
    block = P("block", "dp", None)
    rows = P("dp", "block")
    return jax.shard_map(
        functools.partial(shards, mesh.shape["dp"]),
        mesh=mesh,
        in_specs=(rows, rows) + (block,) * 12,
        out_specs=(rows,) + (block,) * 8,
        check_vma=False,
    )
```

time: 179 us -> 167 us (0.933)
  waiting for transfers between devices: 48.6 us -> 65.6 us
  Pallas kernels: 63.1 us -> 49.3 us
  starting transfers between devices: 57.8 us -> 46.4 us
  local copies, waits for them, and re-layouts: 6.91 us -> 3.33 us
    all_to_all x4, waiting for transfers between devices: 40.6 us -> 51.9 us  [exchange(): return lax.all_to_all(x, 'block', split_axis=0, concat_axis=0, tiled=True)]
    ppermute x12 -> x9, waiting for transfers between devices: 2.36 us -> 8.09 us  [scatter_parts(): lax.ppermute(parts[k], 'dp', [(j, (j + k) % n) for j in range(n)])]
    pallas_call x2, Pallas kernels: 9.27 us -> 3.66 us  [outer_in(): pl.pallas_call(functools.partial(outer_in_kernel, n, owned_c, contract, f...]
    ppermute x9 -> x6, starting transfers between devices: 15.3 us -> 10 us  [gather_parts(): lax.ppermute(part, 'dp', [(j, (j + k) % n) for j in range(n)])]
    unnamed x46 -> x38, local copies, waits for them, and re-layouts: 6.91 us -> 3.33 us
    all_to_all x4, starting transfers between devices: 26.7 us -> 23.3 us  [exchange(): return lax.all_to_all(x, 'block', split_axis=0, concat_axis=0, tiled=True)]
    pallas_call x1, Pallas kernels: 13.6 us -> 10.8 us  [inner_fwd(): pl.pallas_call(functools.partial(inner_fwd_kernel, n), grid=(tokens // tb...]
    ppermute x12 -> x9, starting transfers between devices: 15.7 us -> 13.1 us  [scatter_parts(): lax.ppermute(parts[k], 'dp', [(j, (j + k) % n) for j in range(n)])]
  transfers between devices with their start and end apart: 25 -> 19, of which waited for: 8 -> 14; matrix products, arithmetic and copies ran while one was open for 0% -> 0% of each run, Pallas kernels for 32% -> 26%
where the time goes in v2:
time: 167 us; the launch traced here: 166 us
  waiting for transfers between devices  65.6 us (39%)
  Pallas kernels  49.3 us (30%)
  starting transfers between devices  46.4 us (28%)
  local copies, waits for them, and re-layouts  3.33 us (2%)
    all_to_all x4, waiting for transfers between devices, exchange(): return lax.all_to_all(x, 'block', split_axis=0, concat_axis=0, tiled=True)  51.9 us
    pallas_call x1, Pallas kernels, inner_bwd(): pl.pallas_call(functools.partial(inner_bwd_kernel, n, owned_c), grid=(tok...  24.9 us
    all_to_all x4, starting transfers between devices, exchange(): return lax.all_to_all(x, 'block', split_axis=0, concat_axis=0, tiled=True)  23.3 us
    ppermute x9, starting transfers between devices, scatter_parts(): lax.ppermute(parts[k], 'dp', [(j, (j + k) % n) for j in range(n)])  13.1 us
    pallas_call x1, Pallas kernels, inner_fwd(): pl.pallas_call(functools.partial(inner_fwd_kernel, n), grid=(tokens // tb...  10.8 us
    ppermute x6, starting transfers between devices, gather_parts(): lax.ppermute(part, 'dp', [(j, (j + k) % n) for j in range(n)])  10 us
    ppermute x9, waiting for transfers between devices, scatter_parts(): lax.ppermute(parts[k], 'dp', [(j, (j + k) % n) for j in range(n)])  8.09 us
    ppermute x6, waiting for transfers between devices, gather_parts(): lax.ppermute(part, 'dp', [(j, (j + k) % n) for j in range(n)])  5.63 us
  transfers between devices with their start and end apart: 19, of which 14 were waited for; matrix products, arithmetic and copies ran while one was open for 0% of the time, Pallas kernels for 26%

profile of v2, /device:TPU:0, one launch (start us, length us, event | category | flops | bytes accessed | tf_op | source)
XLA Modules:
  0.0 166.4 jit_solution(10528725111019301597)
XLA Ops:
  3.2 2.7 %collective-permute-start.1 = (bf16[4,32,128]{2,1,0:T(8,128)(2,1)S(1)}, bf16[4,32,128]{2,1,0:T(8,128)(2,1)S(1)}, u32[]{:S(2)}, u32[]{:S(2)}) collective-permute-start(bf16[4,32,128]{2,1,0:T(8,128)(2,1)S(1)} %pad_maximum_fusion.refs_0_), channel_id=1, source_target_pairs={{0,64},{32,96},{64,0},{96,32},{1,65},{33,97},{65,1},{97,33},{2,66}... | collective-permute-start | bytes 98312 | tf_op jit(solution)/shard_map/ppermute | solution.py:45
  9.8 1.8 %shard_map.206 = (bf16[256,4096]{1,0:T(8,128)(2,1)}, bf16[256,256]{1,0:T(8,128)(2,1)S(1)}) custom-call(bf16[4,32,128]{2,1,0:T(8,128)(2,1)S(1)} %pad_maximum_fusion.refs_0_, bf16[4,32,128]{2,1,0:T(8,128)(2,1)S(1)} %collective-permute-done.refs_1_, bf16[4,32,128]{2,1,0:T(8,128)(2,1)S(1)} %collective-permute-done.1.refs_2_, ...), custom_call_target="tpu_custom_call" | custom-call | flops 536870912 | bytes 4194304 | tf_op jit(solution)/shard_map/pallas_call | solution.py:141
  11.7 8.7 %all-to-all-start = ((bf16[32,8,4096]{2,1,0:T(8,128)(2,1)}), bf16[32,8,4096]{2,1,0:T(8,128)(2,1)}, u32[]{:S(2)}, u32[]{:S(2)}) async-start(bf16[32,8,4096]{2,1,0:T(8,128)(2,1)} %bitcast.9), calls=%async_computation | async-start | bytes 4194304 | tf_op jit(solution)/shard_map/all_to_all | solution.py:55
  21.1 3.8 %collective-permute-start.4 = (bf16[6,64,128]{2,1,0:T(8,128)(2,1)S(1)}, bf16[6,64,128]{2,1,0:T(8,128)(2,1)S(1)}, u32[]{:S(2)}, u32[]{:S(2)}) collective-permute-start(bf16[6,64,128]{2,1,0:T(8,128)(2,1)S(1)} %shard_map.207.refs_0_.refs_5_), channel_id=1, source_target_pairs={{0,64},{32,96},{64,0},{96,32},{1,65},{33,97},{65,1},{97,33},{2,66}... | collective-permute-start | bytes 294920 | tf_op jit(solution)/shard_map/ppermute | solution.py:45
  24.9 2.0 %collective-permute-done.3.refs_1_.refs_6_ = bf16[6,64,128]{2,1,0:T(8,128)(2,1)S(1)} collective-permute-done((bf16[6,64,128]{2,1,0:T(8,128)(2,1)S(1)}, bf16[6,64,128]{2,1,0:T(8,128)(2,1)S(1)}, u32[]{:S(2)}, u32[]{:S(2)}) %collective-permute-start.3) | collective-permute-done | bytes 98336 | tf_op jit(solution)/shard_map/ppermute | solution.py:45
  26.9 3.0 %collective-permute-done.4.refs_2_.refs_7_ = bf16[6,64,128]{2,1,0:T(8,128)(2,1)S(1)} collective-permute-done((bf16[6,64,128]{2,1,0:T(8,128)(2,1)S(1)}, bf16[6,64,128]{2,1,0:T(8,128)(2,1)S(1)}, u32[]{:S(2)}, u32[]{:S(2)}) %collective-permute-start.4) | collective-permute-done | bytes 98336 | tf_op jit(solution)/shard_map/ppermute | solution.py:45
  29.9 1.8 %shard_map.209 = (bf16[256,4096]{1,0:T(8,128)(2,1)}, bf16[256,256]{1,0:T(8,128)(2,1)S(1)}) custom-call(bf16[4,32,128]{2,1,0:T(8,128)(2,1)S(1)} %pad_maximum_fusion.refs_0_, bf16[4,32,128]{2,1,0:T(8,128)(2,1)S(1)} %collective-permute-done.refs_1_, bf16[4,32,128]{2,1,0:T(8,128)(2,1)S(1)} %collective-permute-done.1.refs_2_, ...), custom_call_target="tpu_custom_call" | custom-call | flops 536870912 | bytes 4194304 | tf_op jit(solution)/shard_map/pallas_call | solution.py:141
  31.8 18.7 %all-to-all-done = bf16[32,8,4096]{2,1,0:T(8,128)(2,1)} async-done(((bf16[32,8,4096]{2,1,0:T(8,128)(2,1)}), bf16[32,8,4096]{2,1,0:T(8,128)(2,1)}, u32[]{:S(2)}, u32[]{:S(2)}) %all-to-all-start) | async-done | bytes 2097184 | tf_op jit(solution)/shard_map/all_to_all | solution.py:55
  50.5 4.8 %all-to-all-start.2 = ((bf16[32,8,4096]{2,1,0:T(8,128)(2,1)}), bf16[32,8,4096]{2,1,0:T(8,128)(2,1)}, u32[]{:S(2)}, u32[]{:S(2)}) async-start(bf16[32,8,4096]{2,1,0:T(8,128)(2,1)} %bitcast.11), calls=%async_computation.2 | async-start | bytes 4194304 | tf_op jit(solution)/shard_map/all_to_all | solution.py:55
  55.2 10.8 %shard_map.208 = (bf16[256,4096]{1,0:T(8,128)(2,1)}, bf16[2048,256]{1,0:T(8,128)(2,1)}, bf16[256,1024]{1,0:T(8,128)(2,1)}) custom-call(bf16[6,64,128]{2,1,0:T(8,128)(2,1)S(1)} %shard_map.207.refs_0_.refs_5_, bf16[6,64,128]{2,1,0:T(8,128)(2,1)S(1)} %collective-permute-done.3.refs_1_.refs_6_, bf16[6,64,128]{2,1,0:T(8,128)(2,1)S(1)} %collective-permute-done.4.refs_2_.refs_7_, ...), custom_call_target="tpu_custom_call" | custom-call | flops 6442450944 | bytes 4194304 | tf_op jit(solution)/shard_map/pallas_call | solution.py:305
  66.1 19.1 %all-to-all-done.2 = bf16[32,8,4096]{2,1,0:T(8,128)(2,1)} async-done(((bf16[32,8,4096]{2,1,0:T(8,128)(2,1)}), bf16[32,8,4096]{2,1,0:T(8,128)(2,1)}, u32[]{:S(2)}, u32[]{:S(2)}) %all-to-all-start.2) | async-done | bytes 2097184 | tf_op jit(solution)/shard_map/all_to_all | solution.py:55
  85.2 4.9 %all-to-all-start.1 = ((bf16[32,8,4096]{2,1,0:T(8,128)(2,1)}), bf16[32,8,4096]{2,1,0:T(8,128)(2,1)}, u32[]{:S(2)}, u32[]{:S(2)}) async-start(bf16[32,8,4096]{2,1,0:T(8,128)(2,1)} %bitcast.10), calls=%async_computation.1 | async-start | bytes 4194304 | tf_op jit(solution)/shard_map/all_to_all | solution.py:55
  90.1 24.9 %shard_map.211 = (bf16[256,4096]{1,0:T(8,128)(2,1)}, f32[6,64,128]{2,1,0:T(8,128)}, f32[6,64,128]{2,1,0:T(8,128)}, f32[6,64,128]{2,1,0:T(8,128)}, f32[6,64,128]{2,1,0:T(8,128)}) custom-call(bf16[256,4096]{1,0:T(8,128)(2,1)} %bitcast.1.refs_4_.y, bf16[256,4096]{1,0:T(8,128)(2,1)} %bitcast.5.dv, bf16[2048,256]{1,0:T(8,128)(2,1)} %get-tuple-element.44.up2, ...), custom_call_target="tpu_custom_call" | custom-call | flops 17179869184 | bytes 6291456 | tf_op jit(solution)/shard_map/pallas_call | solution.py:384
  115.1 4.8 %all-to-all-done.1 = bf16[32,8,4096]{2,1,0:T(8,128)(2,1)} async-done(((bf16[32,8,4096]{2,1,0:T(8,128)(2,1)}), bf16[32,8,4096]{2,1,0:T(8,128)(2,1)}, u32[]{:S(2)}, u32[]{:S(2)}) %all-to-all-start.1) | async-done | bytes 2097184 | tf_op jit(solution)/shard_map/all_to_all | solution.py:55
  119.9 4.9 %all-to-all-start.3 = ((bf16[32,8,4096]{2,1,0:T(8,128)(2,1)}), bf16[32,8,4096]{2,1,0:T(8,128)(2,1)}, u32[]{:S(2)}, u32[]{:S(2)}) async-start(bf16[32,8,4096]{2,1,0:T(8,128)(2,1)} %bitcast.8), calls=%async_computation.3 | async-start | bytes 4194304 | tf_op jit(solution)/shard_map/all_to_all | solution.py:55
  125.2 3.8 %collective-permute-start.7 = (f32[6,64,128]{2,1,0:T(8,128)S(1)}, f32[6,64,128]{2,1,0:T(8,128)S(1)}, u32[]{:S(2)}, u32[]{:S(2)}) collective-permute-start(f32[6,64,128]{2,1,0:T(8,128)S(1)} %copy-done.17), channel_id=1, source_target_pairs={{0,64},{32,96},{64,0},{96,32},{1,65},{33,97},{65,1},{97,33},{2,66}... | collective-permute-start | bytes 589832 | tf_op jit(solution)/shard_map/ppermute | solution.py:50
  129.0 4.2 %shard_map.210 = (bf16[4096,256]{1,0:T(8,128)(2,1)}, f32[2,32,128]{2,1,0:T(8,128)S(1)}, f32[2,32,128]{2,1,0:T(8,128)S(1)}, f32[2,32,128]{2,1,0:T(8,128)S(1)}, f32[2,32,128]{2,1,0:T(8,128)S(1)}) custom-call(bf16[256,4096]{1,0:T(8,128)(2,1)} %bitcast.3.refs_0_, bf16[4096,256]{1,0:T(8,128)(2,1)S(1)} %copy-done, bf16[256,256]{1,0:T(8,128)(2,1)S(1)} %get-tuple-element.41.refs_2_), custom_call_target="tpu_custom_call" | custom-call | flops 1073741824 | bytes 6291456 | tf_op jit(solution)/shard_map/pallas_call | solution.py:179
  133.2 2.0 %collective-permute-start.10 = (f32[2,32,128]{2,1,0:T(8,128)S(1)}, f32[2,32,128]{2,1,0:T(8,128)S(1)}, u32[]{:S(2)}, u32[]{:S(2)}) collective-permute-start(f32[2,32,128]{2,1,0:T(8,128)S(1)} %get-tuple-element.54), channel_id=1, source_target_pairs={{0,64},{32,96},{64,0},{96,32},{1,65},{33,97},{65,1},{97,33},{2,66}... | collective-permute-start | bytes 98312 | tf_op jit(solution)/shard_map/ppermute | solution.py:50
  135.3 2.6 %collective-permute-start.11 = (f32[2,32,128]{2,1,0:T(8,128)S(1)}, f32[2,32,128]{2,1,0:T(8,128)S(1)}, u32[]{:S(2)}, u32[]{:S(2)}) collective-permute-start(f32[2,32,128]{2,1,0:T(8,128)S(1)} %get-tuple-element.55), channel_id=1, source_target_pairs={{0,96},{32,0},{64,32},{96,64},{1,97},{33,1},{65,33},{97,65},{2,98}... | collective-permute-start | bytes 98312 | tf_op jit(solution)/shard_map/ppermute | solution.py:50
  139.5 3.5 %collective-permute-done.9.refs_1_ = f32[2,32,128]{2,1,0:T(8,128)S(1)} collective-permute-done((f32[2,32,128]{2,1,0:T(8,128)S(1)}, f32[2,32,128]{2,1,0:T(8,128)S(1)}, u32[]{:S(2)}, u32[]{:S(2)}) %collective-permute-start.9) | collective-permute-done | bytes 32800 | tf_op jit(solution)/shard_map/ppermute | solution.py:50
  145.5 9.2 %all-to-all-done.3 = bf16[32,8,4096]{2,1,0:T(8,128)(2,1)} async-done(((bf16[32,8,4096]{2,1,0:T(8,128)(2,1)}), bf16[32,8,4096]{2,1,0:T(8,128)(2,1)}, u32[]{:S(2)}, u32[]{:S(2)}) %all-to-all-start.3) | async-done | bytes 2097184 | tf_op jit(solution)/shard_map/all_to_all | solution.py:55
  154.8 2.9 %shard_map.215 = (f32[2,32,128]{2,1,0:T(8,128)S(1)}, f32[2,32,128]{2,1,0:T(8,128)S(1)}, f32[2,32,128]{2,1,0:T(8,128)S(1)}, f32[2,32,128]{2,1,0:T(8,128)S(1)}) custom-call(bf16[256,4096]{1,0:T(8,128)(2,1)} %bitcast.7.refs_0_, bf16[4096,256]{1,0:T(8,128)(2,1)S(1)} %shard_map.214.refs_1_), custom_call_target="tpu_custom_call" | custom-call | flops 536870912 | bytes 4194304 | tf_op jit(solution)/shard_map/pallas_call | solution.py:218
  158.0 3.8 %collective-permute-start.13 = (f32[2,32,128]{2,1,0:T(8,128)S(1)}, f32[2,32,128]{2,1,0:T(8,128)S(1)}, u32[]{:S(2)}, u32[]{:S(2)}) collective-permute-start(f32[2,32,128]{2,1,0:T(8,128)S(1)} %get-tuple-element.59), channel_id=1, source_target_pairs={{0,64},{32,96},{64,0},{96,32},{1,65},{33,97},{65,1},{97,33},{2,66}... | collective-permute-start | bytes 98312 | tf_op jit(solution)/shard_map/ppermute | solution.py:50
  164.1 1.7 %collective-permute-done.14.refs_3_ = f32[2,32,128]{2,1,0:T(8,128)S(1)} collective-permute-done((f32[2,32,128]{2,1,0:T(8,128)S(1)}, f32[2,32,128]{2,1,0:T(8,128)S(1)}, u32[]{:S(2)}, u32[]{:S(2)}) %collective-permute-start.14) | collective-permute-done | bytes 32800 | tf_op jit(solution)/shard_map/ppermute | solution.py:50
  (66 shorter events, 14.7 us)
Async XLA Ops:
  1.6 7.6 %collective-permute-start = (bf16[4,32,128]{2,1,0:T(8,128)(2,1)S(1)}, bf16[4,32,128]{2,1,0:T(8,128)(2,1)S(1)}, u32[]{:S(2)}, u32[]{:S(2)}) collective-permute-start(bf16[4,32,128]{2,1,0:T(8,128)(2,1)S(1)} %pad_maximum_fusion.refs_0_), channel_id=1, source_target_pairs={{0,32},{32,64},{64,96},{96,0},{1,33},{33,65},{65,97},{97,1},{2,34}... | collective-permute-start | bytes 98312 | tf_op jit(solution)/shard_map/ppermute | solution.py:45
  3.2 6.0 %collective-permute-start.1 = (bf16[4,32,128]{2,1,0:T(8,128)(2,1)S(1)}, bf16[4,32,128]{2,1,0:T(8,128)(2,1)S(1)}, u32[]{:S(2)}, u32[]{:S(2)}) collective-permute-start(bf16[4,32,128]{2,1,0:T(8,128)(2,1)S(1)} %pad_maximum_fusion.refs_0_), channel_id=1, source_target_pairs={{0,64},{32,96},{64,0},{96,32},{1,65},{33,97},{65,1},{97,33},{2,66}... | collective-permute-start | bytes 98312 | tf_op jit(solution)/shard_map/ppermute | solution.py:45
  5.9 3.9 %collective-permute-start.2 = (bf16[4,32,128]{2,1,0:T(8,128)(2,1)S(1)}, bf16[4,32,128]{2,1,0:T(8,128)(2,1)S(1)}, u32[]{:S(2)}, u32[]{:S(2)}) collective-permute-start(bf16[4,32,128]{2,1,0:T(8,128)(2,1)S(1)} %pad_maximum_fusion.refs_0_), channel_id=1, source_target_pairs={{0,96},{32,0},{64,32},{96,64},{1,97},{33,1},{65,33},{97,65},{2,98}... | collective-permute-start | bytes 98312 | tf_op jit(solution)/shard_map/ppermute | solution.py:45
  11.7 18.2 %copy-start = (bf16[4096,256]{1,0:T(8,128)(2,1)S(1)}, bf16[4096,256]{1,0:T(8,128)(2,1)}, u32[]{:S(2)}) copy-start(bf16[4096,256]{1,0:T(8,128)(2,1)} %refs_1_.1) | copy-start | bytes 6291460
  11.7 38.7 %all-to-all-start = ((bf16[32,8,4096]{2,1,0:T(8,128)(2,1)}), bf16[32,8,4096]{2,1,0:T(8,128)(2,1)}, u32[]{:S(2)}, u32[]{:S(2)}) async-start(bf16[32,8,4096]{2,1,0:T(8,128)(2,1)} %bitcast.9), calls=%async_computation | async-start | bytes 4194304 | tf_op jit(solution)/shard_map/all_to_all | solution.py:55
  20.7 6.2 %collective-permute-start.3 = (bf16[6,64,128]{2,1,0:T(8,128)(2,1)S(1)}, bf16[6,64,128]{2,1,0:T(8,128)(2,1)S(1)}, u32[]{:S(2)}, u32[]{:S(2)}) collective-permute-start(bf16[6,64,128]{2,1,0:T(8,128)(2,1)S(1)} %shard_map.207.refs_0_.refs_5_), channel_id=1, source_target_pairs={{0,32},{32,64},{64,96},{96,0},{1,33},{33,65},{65,97},{97,1},{2,34}... | collective-permute-start | bytes 294920 | tf_op jit(solution)/shard_map/ppermute | solution.py:45
  21.1 8.8 %collective-permute-start.4 = (bf16[6,64,128]{2,1,0:T(8,128)(2,1)S(1)}, bf16[6,64,128]{2,1,0:T(8,128)(2,1)S(1)}, u32[]{:S(2)}, u32[]{:S(2)}) collective-permute-start(bf16[6,64,128]{2,1,0:T(8,128)(2,1)S(1)} %shard_map.207.refs_0_.refs_5_), channel_id=1, source_target_pairs={{0,64},{32,96},{64,0},{96,32},{1,65},{33,97},{65,1},{97,33},{2,66}... | collective-permute-start | bytes 294920 | tf_op jit(solution)/shard_map/ppermute | solution.py:45
  24.9 5.0 %collective-permute-start.5 = (bf16[6,64,128]{2,1,0:T(8,128)(2,1)S(1)}, bf16[6,64,128]{2,1,0:T(8,128)(2,1)S(1)}, u32[]{:S(2)}, u32[]{:S(2)}) collective-permute-start(bf16[6,64,128]{2,1,0:T(8,128)(2,1)S(1)} %shard_map.207.refs_0_.refs_5_), channel_id=1, source_target_pairs={{0,96},{32,0},{64,32},{96,64},{1,97},{33,1},{65,33},{97,65},{2,98}... | collective-permute-start | bytes 294920 | tf_op jit(solution)/shard_map/ppermute | solution.py:45
  50.5 34.7 %all-to-all-start.2 = ((bf16[32,8,4096]{2,1,0:T(8,128)(2,1)}), bf16[32,8,4096]{2,1,0:T(8,128)(2,1)}, u32[]{:S(2)}, u32[]{:S(2)}) async-start(bf16[32,8,4096]{2,1,0:T(8,128)(2,1)} %bitcast.11), calls=%async_computation.2 | async-start | bytes 4194304 | tf_op jit(solution)/shard_map/all_to_all | solution.py:55
  85.2 34.7 %all-to-all-start.1 = ((bf16[32,8,4096]{2,1,0:T(8,128)(2,1)}), bf16[32,8,4096]{2,1,0:T(8,128)(2,1)}, u32[]{:S(2)}, u32[]{:S(2)}) async-start(bf16[32,8,4096]{2,1,0:T(8,128)(2,1)} %bitcast.10), calls=%async_computation.1 | async-start | bytes 4194304 | tf_op jit(solution)/shard_map/all_to_all | solution.py:55
  119.9 34.9 %all-to-all-start.3 = ((bf16[32,8,4096]{2,1,0:T(8,128)(2,1)}), bf16[32,8,4096]{2,1,0:T(8,128)(2,1)}, u32[]{:S(2)}, u32[]{:S(2)}) async-start(bf16[32,8,4096]{2,1,0:T(8,128)(2,1)} %bitcast.8), calls=%async_computation.3 | async-start | bytes 4194304 | tf_op jit(solution)/shard_map/all_to_all | solution.py:55
  124.8 13.1 %collective-permute-start.6 = (f32[6,64,128]{2,1,0:T(8,128)S(1)}, f32[6,64,128]{2,1,0:T(8,128)S(1)}, u32[]{:S(2)}, u32[]{:S(2)}) collective-permute-start(f32[6,64,128]{2,1,0:T(8,128)S(1)} %copy-done.18), channel_id=1, source_target_pairs={{0,32},{32,64},{64,96},{96,0},{1,33},{33,65},{65,97},{97,1},{2,34}... | collective-permute-start | bytes 589832 | tf_op jit(solution)/shard_map/ppermute | solution.py:50
  125.2 13.3 %collective-permute-start.7 = (f32[6,64,128]{2,1,0:T(8,128)S(1)}, f32[6,64,128]{2,1,0:T(8,128)S(1)}, u32[]{:S(2)}, u32[]{:S(2)}) collective-permute-start(f32[6,64,128]{2,1,0:T(8,128)S(1)} %copy-done.17), channel_id=1, source_target_pairs={{0,64},{32,96},{64,0},{96,32},{1,65},{33,97},{65,1},{97,33},{2,66}... | collective-permute-start | bytes 589832 | tf_op jit(solution)/shard_map/ppermute | solution.py:50
  129.0 9.5 %collective-permute-start.8 = (f32[6,64,128]{2,1,0:T(8,128)S(1)}, f32[6,64,128]{2,1,0:T(8,128)S(1)}, u32[]{:S(2)}, u32[]{:S(2)}) collective-permute-start(f32[6,64,128]{2,1,0:T(8,128)S(1)} %copy-done.16), channel_id=1, source_target_pairs={{0,96},{32,0},{64,32},{96,64},{1,97},{33,1},{65,33},{97,65},{2,98}... | collective-permute-start | bytes 589832 | tf_op jit(solution)/shard_map/ppermute | solution.py:50
  129.0 14.0 %copy-start.9 = (f32[2,32,128]{2,1,0:T(8,128)S(1)}, f32[2,32,128]{2,1,0:T(8,128)}, u32[]{:S(2)}) copy-start(f32[2,32,128]{2,1,0:T(8,128)} %refs_5_.4) | copy-start | bytes 98308
  129.0 14.0 %copy-start.10 = (f32[2,32,128]{2,1,0:T(8,128)S(1)}, f32[2,32,128]{2,1,0:T(8,128)}, u32[]{:S(2)}) copy-start(f32[2,32,128]{2,1,0:T(8,128)} %refs_4_.6) | copy-start | bytes 98308
  129.0 14.7 %copy-start.2 = (bf16[4096,256]{1,0:T(8,128)(2,1)S(1)}, bf16[4096,256]{1,0:T(8,128)(2,1)}, u32[]{:S(2)}) copy-start(bf16[4096,256]{1,0:T(8,128)(2,1)} %x.3) | copy-start | bytes 6291460
  133.2 6.2 %collective-permute-start.10 = (f32[2,32,128]{2,1,0:T(8,128)S(1)}, f32[2,32,128]{2,1,0:T(8,128)S(1)}, u32[]{:S(2)}, u32[]{:S(2)}) collective-permute-start(f32[2,32,128]{2,1,0:T(8,128)S(1)} %get-tuple-element.54), channel_id=1, source_target_pairs={{0,64},{32,96},{64,0},{96,32},{1,65},{33,97},{65,1},{97,33},{2,66}... | collective-permute-start | bytes 98312 | tf_op jit(solution)/shard_map/ppermute | solution.py:50
  135.3 4.2 %collective-permute-start.11 = (f32[2,32,128]{2,1,0:T(8,128)S(1)}, f32[2,32,128]{2,1,0:T(8,128)S(1)}, u32[]{:S(2)}, u32[]{:S(2)}) collective-permute-start(f32[2,32,128]{2,1,0:T(8,128)S(1)} %get-tuple-element.55), channel_id=1, source_target_pairs={{0,96},{32,0},{64,32},{96,64},{1,97},{33,1},{65,33},{97,65},{2,98}... | collective-permute-start | bytes 98312 | tf_op jit(solution)/shard_map/ppermute | solution.py:50
  137.9 5.1 %collective-permute-start.9 = (f32[2,32,128]{2,1,0:T(8,128)S(1)}, f32[2,32,128]{2,1,0:T(8,128)S(1)}, u32[]{:S(2)}, u32[]{:S(2)}) collective-permute-start(f32[2,32,128]{2,1,0:T(8,128)S(1)} %get-tuple-element.53), channel_id=1, source_target_pairs={{0,32},{32,64},{64,96},{96,0},{1,33},{33,65},{65,97},{97,1},{2,34}... | collective-permute-start | bytes 98312 | tf_op jit(solution)/shard_map/ppermute | solution.py:50
  154.8 11.0 %copy-start.12 = (f32[2,32,128]{2,1,0:T(8,128)S(1)}, f32[2,32,128]{2,1,0:T(8,128)}, u32[]{:S(2)}) copy-start(f32[2,32,128]{2,1,0:T(8,128)} %refs_4_.7) | copy-start | bytes 98308
  157.7 5.2 %collective-permute-start.12 = (f32[2,32,128]{2,1,0:T(8,128)S(1)}, f32[2,32,128]{2,1,0:T(8,128)S(1)}, u32[]{:S(2)}, u32[]{:S(2)}) collective-permute-start(f32[2,32,128]{2,1,0:T(8,128)S(1)} %get-tuple-element.58), channel_id=1, source_target_pairs={{0,32},{32,64},{64,96},{96,0},{1,33},{33,65},{65,97},{97,1},{2,34}... | collective-permute-start | bytes 98312 | tf_op jit(solution)/shard_map/ppermute | solution.py:50
  158.0 6.1 %collective-permute-start.13 = (f32[2,32,128]{2,1,0:T(8,128)S(1)}, f32[2,32,128]{2,1,0:T(8,128)S(1)}, u32[]{:S(2)}, u32[]{:S(2)}) collective-permute-start(f32[2,32,128]{2,1,0:T(8,128)S(1)} %get-tuple-element.59), channel_id=1, source_target_pairs={{0,64},{32,96},{64,0},{96,32},{1,65},{33,97},{65,1},{97,33},{2,66}... | collective-permute-start | bytes 98312 | tf_op jit(solution)/shard_map/ppermute | solution.py:50
  161.9 3.9 %collective-permute-start.14 = (f32[2,32,128]{2,1,0:T(8,128)S(1)}, f32[2,32,128]{2,1,0:T(8,128)S(1)}, u32[]{:S(2)}, u32[]{:S(2)}) collective-permute-start(f32[2,32,128]{2,1,0:T(8,128)S(1)} %get-tuple-element.60), channel_id=1, source_target_pairs={{0,96},{32,0},{64,32},{96,64},{1,97},{33,1},{65,33},{97,65},{2,98}... | collective-permute-start | bytes 98312 | tf_op jit(solution)/shard_map/ppermute | solution.py:50
  (14 other events, 96.0 us)

commit v3 on v2

--- a/solution.py
+++ b/solution.py
@@ -197,14 +197,12 @@
     *parts, held, full, done = refs[-n - 3 :]
     width = full.shape[2]
     pieces = chunks(x.shape[0], count)
-    copies = [pltpu.make_async_copy(z.at[:, cols], held.at[:, cols], done.at[k]) for k, cols in enumerate(pieces)]
+    copies = [pltpu.make_async_copy(z.at[at], held.at[at], done.at[k]) for k, at in enumerate(chunks(z.shape[0], count))]
     for copy in copies:
         copy.start()
-    total = None
-    for copy, cols in zip(copies, pieces):
+    for copy in copies:
         copy.wait()
-        term = dot(held[:, cols], x[cols, :], 1, 0)
-        total = term if total is None else total + term
+    total = dot(held[...], x[...], 1, 0)
     for m in range(owned_m):
         hot = place_m(m, owned_m, owned_c, total.shape[0], width, BF16)
         full[m] = picked(total[:, m * width : (m + 1) * width], hot, 0, 0)

time: 167 us -> 167 us (level)
  no operation moved by 1% of the time
where the time goes in v3:
time: 167 us; the launch traced here: 166 us
  waiting for transfers between devices  65.6 us (39%)
  Pallas kernels  49.1 us (29%)
  starting transfers between devices  46.4 us (28%)
  local copies, waits for them, and re-layouts  3.33 us (2%)
    all_to_all x4, waiting for transfers between devices, exchange(): return lax.all_to_all(x, 'block', split_axis=0, concat_axis=0, tiled=True)  51.9 us
    pallas_call x1, Pallas kernels, inner_bwd(): pl.pallas_call(functools.partial(inner_bwd_kernel, n, owned_c), grid=(tok...  24.9 us
    all_to_all x4, starting transfers between devices, exchange(): return lax.all_to_all(x, 'block', split_axis=0, concat_axis=0, tiled=True)  23.3 us
    ppermute x9, starting transfers between devices, scatter_parts(): lax.ppermute(parts[k], 'dp', [(j, (j + k) % n) for j in range(n)])  13.1 us
    pallas_call x1, Pallas kernels, inner_fwd(): pl.pallas_call(functools.partial(inner_fwd_kernel, n), grid=(tokens // tb...  10.8 us
    ppermute x6, starting transfers between devices, gather_parts(): lax.ppermute(part, 'dp', [(j, (j + k) % n) for j in range(n)])  10 us
    ppermute x9, waiting for transfers between devices, scatter_parts(): lax.ppermute(parts[k], 'dp', [(j, (j + k) % n) for j in range(n)])  8.09 us
    ppermute x6, waiting for transfers between devices, gather_parts(): lax.ppermute(part, 'dp', [(j, (j + k) % n) for j in range(n)])  5.63 us
  transfers between devices with their start and end apart: 19, of which 14 were waited for; matrix products, arithmetic and copies ran while one was open for 0% of the time, Pallas kernels for 26%

profile of v3, /device:TPU:0, one launch (start us, length us, event | category | flops | bytes accessed | tf_op | source)
XLA Modules:
  0.0 166.3 jit_solution(4662491434856161527)
XLA Ops:
  3.2 2.7 %collective-permute-start.1 = (bf16[4,32,128]{2,1,0:T(8,128)(2,1)S(1)}, bf16[4,32,128]{2,1,0:T(8,128)(2,1)S(1)}, u32[]{:S(2)}, u32[]{:S(2)}) collective-permute-start(bf16[4,32,128]{2,1,0:T(8,128)(2,1)S(1)} %pad_maximum_fusion.refs_0_), channel_id=1, source_target_pairs={{0,64},{32,96},{64,0},{96,32},{1,65},{33,97},{65,1},{97,33},{2,66}... | collective-permute-start | bytes 98312 | tf_op jit(solution)/shard_map/ppermute | solution.py:45
  9.8 1.8 %shard_map.206 = (bf16[256,4096]{1,0:T(8,128)(2,1)}, bf16[256,256]{1,0:T(8,128)(2,1)S(1)}) custom-call(bf16[4,32,128]{2,1,0:T(8,128)(2,1)S(1)} %pad_maximum_fusion.refs_0_, bf16[4,32,128]{2,1,0:T(8,128)(2,1)S(1)} %collective-permute-done.refs_1_, bf16[4,32,128]{2,1,0:T(8,128)(2,1)S(1)} %collective-permute-done.1.refs_2_, ...), custom_call_target="tpu_custom_call" | custom-call | flops 536870912 | bytes 4194304 | tf_op jit(solution)/shard_map/pallas_call | solution.py:141
  11.7 8.7 %all-to-all-start = ((bf16[32,8,4096]{2,1,0:T(8,128)(2,1)}), bf16[32,8,4096]{2,1,0:T(8,128)(2,1)}, u32[]{:S(2)}, u32[]{:S(2)}) async-start(bf16[32,8,4096]{2,1,0:T(8,128)(2,1)} %bitcast.9), calls=%async_computation | async-start | bytes 4194304 | tf_op jit(solution)/shard_map/all_to_all | solution.py:55
  21.1 3.8 %collective-permute-start.4 = (bf16[6,64,128]{2,1,0:T(8,128)(2,1)S(1)}, bf16[6,64,128]{2,1,0:T(8,128)(2,1)S(1)}, u32[]{:S(2)}, u32[]{:S(2)}) collective-permute-start(bf16[6,64,128]{2,1,0:T(8,128)(2,1)S(1)} %shard_map.207.refs_0_.refs_5_), channel_id=1, source_target_pairs={{0,64},{32,96},{64,0},{96,32},{1,65},{33,97},{65,1},{97,33},{2,66}... | collective-permute-start | bytes 294920 | tf_op jit(solution)/shard_map/ppermute | solution.py:45
  24.9 2.0 %collective-permute-done.3.refs_1_.refs_6_ = bf16[6,64,128]{2,1,0:T(8,128)(2,1)S(1)} collective-permute-done((bf16[6,64,128]{2,1,0:T(8,128)(2,1)S(1)}, bf16[6,64,128]{2,1,0:T(8,128)(2,1)S(1)}, u32[]{:S(2)}, u32[]{:S(2)}) %collective-permute-start.3) | collective-permute-done | bytes 98336 | tf_op jit(solution)/shard_map/ppermute | solution.py:45
  26.9 3.0 %collective-permute-done.4.refs_2_.refs_7_ = bf16[6,64,128]{2,1,0:T(8,128)(2,1)S(1)} collective-permute-done((bf16[6,64,128]{2,1,0:T(8,128)(2,1)S(1)}, bf16[6,64,128]{2,1,0:T(8,128)(2,1)S(1)}, u32[]{:S(2)}, u32[]{:S(2)}) %collective-permute-start.4) | collective-permute-done | bytes 98336 | tf_op jit(solution)/shard_map/ppermute | solution.py:45
  29.9 1.8 %shard_map.209 = (bf16[256,4096]{1,0:T(8,128)(2,1)}, bf16[256,256]{1,0:T(8,128)(2,1)S(1)}) custom-call(bf16[4,32,128]{2,1,0:T(8,128)(2,1)S(1)} %pad_maximum_fusion.refs_0_, bf16[4,32,128]{2,1,0:T(8,128)(2,1)S(1)} %collective-permute-done.refs_1_, bf16[4,32,128]{2,1,0:T(8,128)(2,1)S(1)} %collective-permute-done.1.refs_2_, ...), custom_call_target="tpu_custom_call" | custom-call | flops 536870912 | bytes 4194304 | tf_op jit(solution)/shard_map/pallas_call | solution.py:141
  31.8 18.7 %all-to-all-done = bf16[32,8,4096]{2,1,0:T(8,128)(2,1)} async-done(((bf16[32,8,4096]{2,1,0:T(8,128)(2,1)}), bf16[32,8,4096]{2,1,0:T(8,128)(2,1)}, u32[]{:S(2)}, u32[]{:S(2)}) %all-to-all-start) | async-done | bytes 2097184 | tf_op jit(solution)/shard_map/all_to_all | solution.py:55
  50.5 4.8 %all-to-all-start.2 = ((bf16[32,8,4096]{2,1,0:T(8,128)(2,1)}), bf16[32,8,4096]{2,1,0:T(8,128)(2,1)}, u32[]{:S(2)}, u32[]{:S(2)}) async-start(bf16[32,8,4096]{2,1,0:T(8,128)(2,1)} %bitcast.11), calls=%async_computation.2 | async-start | bytes 4194304 | tf_op jit(solution)/shard_map/all_to_all | solution.py:55
  55.2 10.8 %shard_map.208 = (bf16[256,4096]{1,0:T(8,128)(2,1)}, bf16[2048,256]{1,0:T(8,128)(2,1)}, bf16[256,1024]{1,0:T(8,128)(2,1)}) custom-call(bf16[6,64,128]{2,1,0:T(8,128)(2,1)S(1)} %shard_map.207.refs_0_.refs_5_, bf16[6,64,128]{2,1,0:T(8,128)(2,1)S(1)} %collective-permute-done.3.refs_1_.refs_6_, bf16[6,64,128]{2,1,0:T(8,128)(2,1)S(1)} %collective-permute-done.4.refs_2_.refs_7_, ...), custom_call_target="tpu_custom_call" | custom-call | flops 6442450944 | bytes 4194304 | tf_op jit(solution)/shard_map/pallas_call | solution.py:303
  66.1 19.1 %all-to-all-done.2 = bf16[32,8,4096]{2,1,0:T(8,128)(2,1)} async-done(((bf16[32,8,4096]{2,1,0:T(8,128)(2,1)}), bf16[32,8,4096]{2,1,0:T(8,128)(2,1)}, u32[]{:S(2)}, u32[]{:S(2)}) %all-to-all-start.2) | async-done | bytes 2097184 | tf_op jit(solution)/shard_map/all_to_all | solution.py:55
  85.2 4.9 %all-to-all-start.1 = ((bf16[32,8,4096]{2,1,0:T(8,128)(2,1)}), bf16[32,8,4096]{2,1,0:T(8,128)(2,1)}, u32[]{:S(2)}, u32[]{:S(2)}) async-start(bf16[32,8,4096]{2,1,0:T(8,128)(2,1)} %bitcast.10), calls=%async_computation.1 | async-start | bytes 4194304 | tf_op jit(solution)/shard_map/all_to_all | solution.py:55
  90.1 24.9 %shard_map.211 = (bf16[256,4096]{1,0:T(8,128)(2,1)}, f32[6,64,128]{2,1,0:T(8,128)}, f32[6,64,128]{2,1,0:T(8,128)}, f32[6,64,128]{2,1,0:T(8,128)}, f32[6,64,128]{2,1,0:T(8,128)}) custom-call(bf16[256,4096]{1,0:T(8,128)(2,1)} %bitcast.1.refs_4_.y, bf16[256,4096]{1,0:T(8,128)(2,1)} %bitcast.5.dv, bf16[2048,256]{1,0:T(8,128)(2,1)} %get-tuple-element.44.up2, ...), custom_call_target="tpu_custom_call" | custom-call | flops 17179869184 | bytes 6291456 | tf_op jit(solution)/shard_map/pallas_call | solution.py:382
  115.1 4.8 %all-to-all-done.1 = bf16[32,8,4096]{2,1,0:T(8,128)(2,1)} async-done(((bf16[32,8,4096]{2,1,0:T(8,128)(2,1)}), bf16[32,8,4096]{2,1,0:T(8,128)(2,1)}, u32[]{:S(2)}, u32[]{:S(2)}) %all-to-all-start.1) | async-done | bytes 2097184 | tf_op jit(solution)/shard_map/all_to_all | solution.py:55
  119.9 4.9 %all-to-all-start.3 = ((bf16[32,8,4096]{2,1,0:T(8,128)(2,1)}), bf16[32,8,4096]{2,1,0:T(8,128)(2,1)}, u32[]{:S(2)}, u32[]{:S(2)}) async-start(bf16[32,8,4096]{2,1,0:T(8,128)(2,1)} %bitcast.8), calls=%async_computation.3 | async-start | bytes 4194304 | tf_op jit(solution)/shard_map/all_to_all | solution.py:55
  125.2 3.8 %collective-permute-start.7 = (f32[6,64,128]{2,1,0:T(8,128)S(1)}, f32[6,64,128]{2,1,0:T(8,128)S(1)}, u32[]{:S(2)}, u32[]{:S(2)}) collective-permute-start(f32[6,64,128]{2,1,0:T(8,128)S(1)} %copy-done.17), channel_id=1, source_target_pairs={{0,64},{32,96},{64,0},{96,32},{1,65},{33,97},{65,1},{97,33},{2,66}... | collective-permute-start | bytes 589832 | tf_op jit(solution)/shard_map/ppermute | solution.py:50
  129.0 4.2 %shard_map.210 = (bf16[4096,256]{1,0:T(8,128)(2,1)}, f32[2,32,128]{2,1,0:T(8,128)S(1)}, f32[2,32,128]{2,1,0:T(8,128)S(1)}, f32[2,32,128]{2,1,0:T(8,128)S(1)}, f32[2,32,128]{2,1,0:T(8,128)S(1)}) custom-call(bf16[256,4096]{1,0:T(8,128)(2,1)} %bitcast.3.refs_0_, bf16[4096,256]{1,0:T(8,128)(2,1)S(1)} %copy-done, bf16[256,256]{1,0:T(8,128)(2,1)S(1)} %get-tuple-element.41.refs_2_), custom_call_target="tpu_custom_call" | custom-call | flops 1073741824 | bytes 6291456 | tf_op jit(solution)/shard_map/pallas_call | solution.py:179
  133.2 2.0 %collective-permute-start.10 = (f32[2,32,128]{2,1,0:T(8,128)S(1)}, f32[2,32,128]{2,1,0:T(8,128)S(1)}, u32[]{:S(2)}, u32[]{:S(2)}) collective-permute-start(f32[2,32,128]{2,1,0:T(8,128)S(1)} %get-tuple-element.54), channel_id=1, source_target_pairs={{0,64},{32,96},{64,0},{96,32},{1,65},{33,97},{65,1},{97,33},{2,66}... | collective-permute-start | bytes 98312 | tf_op jit(solution)/shard_map/ppermute | solution.py:50
  135.3 2.6 %collective-permute-start.11 = (f32[2,32,128]{2,1,0:T(8,128)S(1)}, f32[2,32,128]{2,1,0:T(8,128)S(1)}, u32[]{:S(2)}, u32[]{:S(2)}) collective-permute-start(f32[2,32,128]{2,1,0:T(8,128)S(1)} %get-tuple-element.55), channel_id=1, source_target_pairs={{0,96},{32,0},{64,32},{96,64},{1,97},{33,1},{65,33},{97,65},{2,98}... | collective-permute-start | bytes 98312 | tf_op jit(solution)/shard_map/ppermute | solution.py:50
  139.5 3.5 %collective-permute-done.9.refs_1_ = f32[2,32,128]{2,1,0:T(8,128)S(1)} collective-permute-done((f32[2,32,128]{2,1,0:T(8,128)S(1)}, f32[2,32,128]{2,1,0:T(8,128)S(1)}, u32[]{:S(2)}, u32[]{:S(2)}) %collective-permute-start.9) | collective-permute-done | bytes 32800 | tf_op jit(solution)/shard_map/ppermute | solution.py:50
  145.5 9.2 %all-to-all-done.3 = bf16[32,8,4096]{2,1,0:T(8,128)(2,1)} async-done(((bf16[32,8,4096]{2,1,0:T(8,128)(2,1)}), bf16[32,8,4096]{2,1,0:T(8,128)(2,1)}, u32[]{:S(2)}, u32[]{:S(2)}) %all-to-all-start.3) | async-done | bytes 2097184 | tf_op jit(solution)/shard_map/all_to_all | solution.py:55
  154.8 2.7 %shard_map.215 = (f32[2,32,128]{2,1,0:T(8,128)S(1)}, f32[2,32,128]{2,1,0:T(8,128)S(1)}, f32[2,32,128]{2,1,0:T(8,128)S(1)}, f32[2,32,128]{2,1,0:T(8,128)S(1)}) custom-call(bf16[256,4096]{1,0:T(8,128)(2,1)} %bitcast.7.refs_0_, bf16[4096,256]{1,0:T(8,128)(2,1)S(1)} %shard_map.214.refs_1_), custom_call_target="tpu_custom_call" | custom-call | flops 536870912 | bytes 4194304 | tf_op jit(solution)/shard_map/pallas_call | solution.py:216
  157.9 3.8 %collective-permute-start.13 = (f32[2,32,128]{2,1,0:T(8,128)S(1)}, f32[2,32,128]{2,1,0:T(8,128)S(1)}, u32[]{:S(2)}, u32[]{:S(2)}) collective-permute-start(f32[2,32,128]{2,1,0:T(8,128)S(1)} %get-tuple-element.59), channel_id=1, source_target_pairs={{0,64},{32,96},{64,0},{96,32},{1,65},{33,97},{65,1},{97,33},{2,66}... | collective-permute-start | bytes 98312 | tf_op jit(solution)/shard_map/ppermute | solution.py:50
  163.9 1.7 %collective-permute-done.14.refs_3_ = f32[2,32,128]{2,1,0:T(8,128)S(1)} collective-permute-done((f32[2,32,128]{2,1,0:T(8,128)S(1)}, f32[2,32,128]{2,1,0:T(8,128)S(1)}, u32[]{:S(2)}, u32[]{:S(2)}) %collective-permute-start.14) | collective-permute-done | bytes 32800 | tf_op jit(solution)/shard_map/ppermute | solution.py:50
  (66 shorter events, 14.7 us)
Async XLA Ops:
  1.6 7.6 %collective-permute-start = (bf16[4,32,128]{2,1,0:T(8,128)(2,1)S(1)}, bf16[4,32,128]{2,1,0:T(8,128)(2,1)S(1)}, u32[]{:S(2)}, u32[]{:S(2)}) collective-permute-start(bf16[4,32,128]{2,1,0:T(8,128)(2,1)S(1)} %pad_maximum_fusion.refs_0_), channel_id=1, source_target_pairs={{0,32},{32,64},{64,96},{96,0},{1,33},{33,65},{65,97},{97,1},{2,34}... | collective-permute-start | bytes 98312 | tf_op jit(solution)/shard_map/ppermute | solution.py:45
  3.2 6.0 %collective-permute-start.1 = (bf16[4,32,128]{2,1,0:T(8,128)(2,1)S(1)}, bf16[4,32,128]{2,1,0:T(8,128)(2,1)S(1)}, u32[]{:S(2)}, u32[]{:S(2)}) collective-permute-start(bf16[4,32,128]{2,1,0:T(8,128)(2,1)S(1)} %pad_maximum_fusion.refs_0_), channel_id=1, source_target_pairs={{0,64},{32,96},{64,0},{96,32},{1,65},{33,97},{65,1},{97,33},{2,66}... | collective-permute-start | bytes 98312 | tf_op jit(solution)/shard_map/ppermute | solution.py:45
  5.9 3.9 %collective-permute-start.2 = (bf16[4,32,128]{2,1,0:T(8,128)(2,1)S(1)}, bf16[4,32,128]{2,1,0:T(8,128)(2,1)S(1)}, u32[]{:S(2)}, u32[]{:S(2)}) collective-permute-start(bf16[4,32,128]{2,1,0:T(8,128)(2,1)S(1)} %pad_maximum_fusion.refs_0_), channel_id=1, source_target_pairs={{0,96},{32,0},{64,32},{96,64},{1,97},{33,1},{65,33},{97,65},{2,98}... | collective-permute-start | bytes 98312 | tf_op jit(solution)/shard_map/ppermute | solution.py:45
  11.7 18.2 %copy-start = (bf16[4096,256]{1,0:T(8,128)(2,1)S(1)}, bf16[4096,256]{1,0:T(8,128)(2,1)}, u32[]{:S(2)}) copy-start(bf16[4096,256]{1,0:T(8,128)(2,1)} %refs_1_.1) | copy-start | bytes 6291460
  11.7 38.7 %all-to-all-start = ((bf16[32,8,4096]{2,1,0:T(8,128)(2,1)}), bf16[32,8,4096]{2,1,0:T(8,128)(2,1)}, u32[]{:S(2)}, u32[]{:S(2)}) async-start(bf16[32,8,4096]{2,1,0:T(8,128)(2,1)} %bitcast.9), calls=%async_computation | async-start | bytes 4194304 | tf_op jit(solution)/shard_map/all_to_all | solution.py:55
  20.7 6.2 %collective-permute-start.3 = (bf16[6,64,128]{2,1,0:T(8,128)(2,1)S(1)}, bf16[6,64,128]{2,1,0:T(8,128)(2,1)S(1)}, u32[]{:S(2)}, u32[]{:S(2)}) collective-permute-start(bf16[6,64,128]{2,1,0:T(8,128)(2,1)S(1)} %shard_map.207.refs_0_.refs_5_), channel_id=1, source_target_pairs={{0,32},{32,64},{64,96},{96,0},{1,33},{33,65},{65,97},{97,1},{2,34}... | collective-permute-start | bytes 294920 | tf_op jit(solution)/shard_map/ppermute | solution.py:45
  21.1 8.8 %collective-permute-start.4 = (bf16[6,64,128]{2,1,0:T(8,128)(2,1)S(1)}, bf16[6,64,128]{2,1,0:T(8,128)(2,1)S(1)}, u32[]{:S(2)}, u32[]{:S(2)}) collective-permute-start(bf16[6,64,128]{2,1,0:T(8,128)(2,1)S(1)} %shard_map.207.refs_0_.refs_5_), channel_id=1, source_target_pairs={{0,64},{32,96},{64,0},{96,32},{1,65},{33,97},{65,1},{97,33},{2,66}... | collective-permute-start | bytes 294920 | tf_op jit(solution)/shard_map/ppermute | solution.py:45
  24.9 5.0 %collective-permute-start.5 = (bf16[6,64,128]{2,1,0:T(8,128)(2,1)S(1)}, bf16[6,64,128]{2,1,0:T(8,128)(2,1)S(1)}, u32[]{:S(2)}, u32[]{:S(2)}) collective-permute-start(bf16[6,64,128]{2,1,0:T(8,128)(2,1)S(1)} %shard_map.207.refs_0_.refs_5_), channel_id=1, source_target_pairs={{0,96},{32,0},{64,32},{96,64},{1,97},{33,1},{65,33},{97,65},{2,98}... | collective-permute-start | bytes 294920 | tf_op jit(solution)/shard_map/ppermute | solution.py:45
  50.5 34.7 %all-to-all-start.2 = ((bf16[32,8,4096]{2,1,0:T(8,128)(2,1)}), bf16[32,8,4096]{2,1,0:T(8,128)(2,1)}, u32[]{:S(2)}, u32[]{:S(2)}) async-start(bf16[32,8,4096]{2,1,0:T(8,128)(2,1)} %bitcast.11), calls=%async_computation.2 | async-start | bytes 4194304 | tf_op jit(solution)/shard_map/all_to_all | solution.py:55
  85.2 34.7 %all-to-all-start.1 = ((bf16[32,8,4096]{2,1,0:T(8,128)(2,1)}), bf16[32,8,4096]{2,1,0:T(8,128)(2,1)}, u32[]{:S(2)}, u32[]{:S(2)}) async-start(bf16[32,8,4096]{2,1,0:T(8,128)(2,1)} %bitcast.10), calls=%async_computation.1 | async-start | bytes 4194304 | tf_op jit(solution)/shard_map/all_to_all | solution.py:55
  119.9 34.9 %all-to-all-start.3 = ((bf16[32,8,4096]{2,1,0:T(8,128)(2,1)}), bf16[32,8,4096]{2,1,0:T(8,128)(2,1)}, u32[]{:S(2)}, u32[]{:S(2)}) async-start(bf16[32,8,4096]{2,1,0:T(8,128)(2,1)} %bitcast.8), calls=%async_computation.3 | async-start | bytes 4194304 | tf_op jit(solution)/shard_map/all_to_all | solution.py:55
  124.8 13.1 %collective-permute-start.6 = (f32[6,64,128]{2,1,0:T(8,128)S(1)}, f32[6,64,128]{2,1,0:T(8,128)S(1)}, u32[]{:S(2)}, u32[]{:S(2)}) collective-permute-start(f32[6,64,128]{2,1,0:T(8,128)S(1)} %copy-done.18), channel_id=1, source_target_pairs={{0,32},{32,64},{64,96},{96,0},{1,33},{33,65},{65,97},{97,1},{2,34}... | collective-permute-start | bytes 589832 | tf_op jit(solution)/shard_map/ppermute | solution.py:50
  125.2 13.3 %collective-permute-start.7 = (f32[6,64,128]{2,1,0:T(8,128)S(1)}, f32[6,64,128]{2,1,0:T(8,128)S(1)}, u32[]{:S(2)}, u32[]{:S(2)}) collective-permute-start(f32[6,64,128]{2,1,0:T(8,128)S(1)} %copy-done.17), channel_id=1, source_target_pairs={{0,64},{32,96},{64,0},{96,32},{1,65},{33,97},{65,1},{97,33},{2,66}... | collective-permute-start | bytes 589832 | tf_op jit(solution)/shard_map/ppermute | solution.py:50
  129.0 9.5 %collective-permute-start.8 = (f32[6,64,128]{2,1,0:T(8,128)S(1)}, f32[6,64,128]{2,1,0:T(8,128)S(1)}, u32[]{:S(2)}, u32[]{:S(2)}) collective-permute-start(f32[6,64,128]{2,1,0:T(8,128)S(1)} %copy-done.16), channel_id=1, source_target_pairs={{0,96},{32,0},{64,32},{96,64},{1,97},{33,1},{65,33},{97,65},{2,98}... | collective-permute-start | bytes 589832 | tf_op jit(solution)/shard_map/ppermute | solution.py:50
  129.0 14.0 %copy-start.9 = (f32[2,32,128]{2,1,0:T(8,128)S(1)}, f32[2,32,128]{2,1,0:T(8,128)}, u32[]{:S(2)}) copy-start(f32[2,32,128]{2,1,0:T(8,128)} %refs_5_.4) | copy-start | bytes 98308
  129.0 14.0 %copy-start.10 = (f32[2,32,128]{2,1,0:T(8,128)S(1)}, f32[2,32,128]{2,1,0:T(8,128)}, u32[]{:S(2)}) copy-start(f32[2,32,128]{2,1,0:T(8,128)} %refs_4_.6) | copy-start | bytes 98308
  129.0 14.7 %copy-start.2 = (bf16[4096,256]{1,0:T(8,128)(2,1)S(1)}, bf16[4096,256]{1,0:T(8,128)(2,1)}, u32[]{:S(2)}) copy-start(bf16[4096,256]{1,0:T(8,128)(2,1)} %x.3) | copy-start | bytes 6291460
  133.2 6.2 %collective-permute-start.10 = (f32[2,32,128]{2,1,0:T(8,128)S(1)}, f32[2,32,128]{2,1,0:T(8,128)S(1)}, u32[]{:S(2)}, u32[]{:S(2)}) collective-permute-start(f32[2,32,128]{2,1,0:T(8,128)S(1)} %get-tuple-element.54), channel_id=1, source_target_pairs={{0,64},{32,96},{64,0},{96,32},{1,65},{33,97},{65,1},{97,33},{2,66}... | collective-permute-start | bytes 98312 | tf_op jit(solution)/shard_map/ppermute | solution.py:50
  135.3 4.2 %collective-permute-start.11 = (f32[2,32,128]{2,1,0:T(8,128)S(1)}, f32[2,32,128]{2,1,0:T(8,128)S(1)}, u32[]{:S(2)}, u32[]{:S(2)}) collective-permute-start(f32[2,32,128]{2,1,0:T(8,128)S(1)} %get-tuple-element.55), channel_id=1, source_target_pairs={{0,96},{32,0},{64,32},{96,64},{1,97},{33,1},{65,33},{97,65},{2,98}... | collective-permute-start | bytes 98312 | tf_op jit(solution)/shard_map/ppermute | solution.py:50
  137.9 5.1 %collective-permute-start.9 = (f32[2,32,128]{2,1,0:T(8,128)S(1)}, f32[2,32,128]{2,1,0:T(8,128)S(1)}, u32[]{:S(2)}, u32[]{:S(2)}) collective-permute-start(f32[2,32,128]{2,1,0:T(8,128)S(1)} %get-tuple-element.53), channel_id=1, source_target_pairs={{0,32},{32,64},{64,96},{96,0},{1,33},{33,65},{65,97},{97,1},{2,34}... | collective-permute-start | bytes 98312 | tf_op jit(solution)/shard_map/ppermute | solution.py:50
  154.8 10.9 %copy-start.12 = (f32[2,32,128]{2,1,0:T(8,128)S(1)}, f32[2,32,128]{2,1,0:T(8,128)}, u32[]{:S(2)}) copy-start(f32[2,32,128]{2,1,0:T(8,128)} %refs_4_.7) | copy-start | bytes 98308
  157.5 5.2 %collective-permute-start.12 = (f32[2,32,128]{2,1,0:T(8,128)S(1)}, f32[2,32,128]{2,1,0:T(8,128)S(1)}, u32[]{:S(2)}, u32[]{:S(2)}) collective-permute-start(f32[2,32,128]{2,1,0:T(8,128)S(1)} %get-tuple-element.58), channel_id=1, source_target_pairs={{0,32},{32,64},{64,96},{96,0},{1,33},{33,65},{65,97},{97,1},{2,34}... | collective-permute-start | bytes 98312 | tf_op jit(solution)/shard_map/ppermute | solution.py:50
  157.9 6.1 %collective-permute-start.13 = (f32[2,32,128]{2,1,0:T(8,128)S(1)}, f32[2,32,128]{2,1,0:T(8,128)S(1)}, u32[]{:S(2)}, u32[]{:S(2)}) collective-permute-start(f32[2,32,128]{2,1,0:T(8,128)S(1)} %get-tuple-element.59), channel_id=1, source_target_pairs={{0,64},{32,96},{64,0},{96,32},{1,65},{33,97},{65,1},{97,33},{2,66}... | collective-permute-start | bytes 98312 | tf_op jit(solution)/shard_map/ppermute | solution.py:50
  161.7 3.9 %collective-permute-start.14 = (f32[2,32,128]{2,1,0:T(8,128)S(1)}, f32[2,32,128]{2,1,0:T(8,128)S(1)}, u32[]{:S(2)}, u32[]{:S(2)}) collective-permute-start(f32[2,32,128]{2,1,0:T(8,128)S(1)} %get-tuple-element.60), channel_id=1, source_target_pairs={{0,96},{32,0},{64,32},{96,64},{1,97},{33,1},{65,33},{97,65},{2,98}... | collective-permute-start | bytes 98312 | tf_op jit(solution)/shard_map/ppermute | solution.py:50
  (14 other events, 95.8 us)
